TPU v7x, 32 devices: a whole 2x2x4 slice. The times are simulated.
32 devices in a mesh: req: 16 (over z, y, x), head: 2 (over core).
Axes of the slice: x: 2, y: 2, z: 4, core: 2. Of those that a mesh axis runs over, the one named last changes fastest.
Arguments:
- verify_x: bfloat16 [16, 5, 2048], P('req'), may hold values from -6 to 6
- prefill_x: bfloat16 [4096, 2048], P('req'), may hold values from -6 to 6
- attn_gain: float32 [2048], replicated, may hold values from 0.25 to 1.75
- w_query: bfloat16 [2048, 2048], P(None, 'head'), may hold values from -0.125 to 0.125
- w_keyval: bfloat16 [2048, 1024], P(None, 'head'), may hold values from -0.125 to 0.125
- qk_gain: float32 [2, 256], replicated, may hold values from 0.25 to 8
- w_out: bfloat16 [2048, 2048], P('head'), may hold values from -0.125 to 0.125
- post_gain: float32 [2048], replicated, may hold values from 0.1 to 1.9
- page_pool: bfloat16 [1024, 16, 1024], P('req', None, 'head'), may hold values from -6 to 6
- outbound: int32 [16, 16], P('req'), may hold values from -1 to 63, as said below
- page_table: int32 [16, 64], P('req'), may hold values from 0 to 79, as said below
- cache_len: int32 [16], P('req'), may hold values from 1 to 1024, as said below
- prompt_len: int32 [16, 4], P('req'), may hold values from 1 to 128, 256 in all within a row
- accepted: int32 [16], P('req'), may hold values from 0 to 5
Outputs:
- verify_out: bfloat16 [16, 5, 2048], P('req', None, 'head')
- prefill_out: bfloat16 [4096, 2048], P('req', 'head')
- verify_kv: bfloat16 [16, 5, 1024], P('req', None, 'head')
- prefill_kv: bfloat16 [4096, 1024], P('req', 'head')
Inputs may be any that keep to these rules, and one draw needn't show every extreme that they name: `outbound`: row s names a page of device s's pool for every device d other than s; the entry at d = s is -1. `page_table`: an entry below 64 names a page of the device's own pool; an entry 64 + s names the page received from device s, s never the device itself. `cache_len`: some request has exactly 1024 cached tokens.
All inputs are finite; a program needn't handle non-finite values.
Results may differ from a plain program's by a relative error of at most 0.015.
The roundings to bfloat16 on the way count: a program that leaves them out, or rounds other values in their place, can miss the bound.
Values may be sent and summed in bfloat16 or wider, within the bound.
A program may use at most 64 MiB of HBM per device.

v0:
```python
import jax
import jax.numpy as jnp
from jax import lax
from jax.sharding import PartitionSpec as P

HEAD = 256


eps_norm = 1e-06
rope_base = 1000000.0
neg_large = -1e30


def rms_scale(values):
    return values * lax.rsqrt(jnp.mean(values * values, axis=-1, keepdims=True) + eps_norm)


def rotate(values, position):
    half_dim = values.shape[-1] // 2
    inv_freq = rope_base ** (-(jnp.arange(half_dim, dtype=jnp.float32) * 2.0) / values.shape[-1])
    angles = position[:, None, None] * inv_freq[None, None, :]
    cosine = jnp.cos(angles)
    sine_part = jnp.sin(angles)
    first = values[..., :half_dim]
    second = values[..., half_dim:]
    return jnp.concatenate(
        [first * cosine - second * sine_part, second * cosine + first * sine_part], axis=-1
    )


def project(hidden_rows, attn_gain, w_query, w_keyval, qk_gain, position):
    row_count = hidden_rows.shape[0]
    normed = (rms_scale(hidden_rows.astype(jnp.float32)) * attn_gain).astype(jnp.bfloat16)
    query_rows = jnp.dot(normed, w_query, preferred_element_type=jnp.float32).reshape(
        row_count, -1, HEAD
    )
    query_rows = rotate(rms_scale(query_rows) * qk_gain[0], position).astype(jnp.bfloat16)
    keyval = jnp.dot(normed, w_keyval, preferred_element_type=jnp.float32).reshape(
        row_count, -1, 2, HEAD
    )
    key_rows = rotate(rms_scale(keyval[:, :, 0]) * qk_gain[1], position).astype(jnp.bfloat16)
    value_rows = rms_scale(keyval[:, :, 1]).astype(jnp.bfloat16)
    return (query_rows, key_rows, value_rows)


def attend(query_rows, key_rows, value_rows, allowed):
    row_count = query_rows.shape[0]
    groups = key_rows.shape[1]
    grouped = query_rows.reshape(row_count, groups, -1, HEAD)
    scores = jnp.einsum("tgqe,jge->gqtj", grouped, key_rows, preferred_element_type=jnp.float32)
    scores = jnp.where(allowed[None, None], scores, neg_large)
    peak_score = jnp.max(scores, axis=-1, keepdims=True)
    weights = jnp.exp(scores - peak_score)
    denom_sum = jnp.sum(weights, axis=-1, keepdims=True)
    attn_probs = (weights / denom_sum).astype(jnp.bfloat16)
    mixed_heads = jnp.einsum(
        "gqtj,jge->tgqe", attn_probs, value_rows, preferred_element_type=jnp.float32
    )
    return mixed_heads.reshape(row_count, -1).astype(jnp.bfloat16)


def prompt_layout(lengths, row_count):
    prompt_ends = jnp.cumsum(lengths)
    row_index = jnp.arange(row_count, dtype=jnp.int32)
    segment = jnp.sum((row_index[:, None] >= prompt_ends[None, :]).astype(jnp.int32), axis=1)
    starts = prompt_ends - lengths
    which = segment[:, None] == jnp.arange(lengths.shape[0], dtype=jnp.int32)[None, :]
    start_row = jnp.sum(jnp.where(which, starts[None, :], 0), axis=1)
    position = (row_index - start_row).astype(jnp.float32)
    allowed = (segment[:, None] == segment[None, :]) & (row_index[None, :] <= row_index[:, None])
    return (position, allowed)


def on_device(
    verify_x,
    prefill_x,
    attn_gain,
    w_query,
    w_keyval,
    qk_gain,
    w_out,
    post_gain,
    page_pool,
    outbound,
    page_table,
    cache_len,
    prompt_len,
    accepted,
):
    req_count, draft_len, width = verify_x.shape
    pref_rows = prefill_x.shape[0]
    sent_page = outbound[0]
    outgoing = jnp.take(page_pool, jnp.clip(sent_page, 0, page_pool.shape[0] - 1), axis=0)
    outgoing = jnp.where((sent_page >= 0)[:, None, None], outgoing, jnp.zeros_like(outgoing))
    arrived = lax.all_to_all(outgoing, "req", split_axis=0, concat_axis=0, tiled=True)
    pool_now = jnp.concatenate([page_pool, arrived], axis=0)
    verify_pos = (
        (cache_len[:, None] + jnp.arange(draft_len, dtype=jnp.int32)[None, :])
        .astype(jnp.float32)
        .reshape(-1)
    )
    prefill_pos, prefill_allowed = prompt_layout(prompt_len[0], pref_rows)
    all_rows = jnp.concatenate([verify_x.reshape(-1, width), prefill_x], axis=0)
    position = jnp.concatenate([verify_pos, prefill_pos], axis=0)
    query_rows, key_rows, value_rows = project(
        all_rows, attn_gain, w_query, w_keyval, qk_gain, position
    )
    groups = key_rows.shape[1]
    verify_count = req_count * draft_len

    def verify_one(query_part, key_part, value_part, page_list, length):
        cached = jnp.take(pool_now, page_list, axis=0).reshape(-1, groups, 2, HEAD)
        cache_rows = cached.shape[0]
        all_keys = jnp.concatenate([cached[:, :, 0], key_part], axis=0)
        all_values = jnp.concatenate([cached[:, :, 1], value_part], axis=0)
        slot = jnp.arange(cache_rows + draft_len, dtype=jnp.int32)
        step_index = jnp.arange(draft_len, dtype=jnp.int32)
        allowed = jnp.where(
            slot[None, :] < cache_rows,
            slot[None, :] < length,
            slot[None, :] - cache_rows <= step_index[:, None],
        )
        return attend(query_part, all_keys, all_values, allowed)

    verify_attn = jax.vmap(verify_one)(
        query_rows[:verify_count].reshape(req_count, draft_len, -1, HEAD),
        key_rows[:verify_count].reshape(req_count, draft_len, groups, HEAD),
        value_rows[:verify_count].reshape(req_count, draft_len, groups, HEAD),
        page_table,
        cache_len,
    )
    prefill_attn = attend(
        query_rows[verify_count:],
        key_rows[verify_count:],
        value_rows[verify_count:],
        prefill_allowed,
    )
    all_attn = jnp.concatenate([verify_attn.reshape(verify_count, -1), prefill_attn], axis=0)
    partial_rows = jnp.dot(all_attn, w_out, preferred_element_type=jnp.float32)
    half_cols = width // lax.axis_size("head")
    offset = lax.axis_index("head") * half_cols
    summed = lax.psum(partial_rows, "head")
    own_part = lax.dynamic_slice_in_dim(rms_scale(summed), offset, half_cols, 1)
    residual = lax.dynamic_slice_in_dim(all_rows, offset, half_cols, 1).astype(jnp.float32)
    gain_part = lax.dynamic_slice_in_dim(post_gain, offset, half_cols, 0)
    final = (residual + own_part * gain_part).astype(jnp.bfloat16)
    verify_out = final[:verify_count].reshape(req_count, draft_len, half_cols)
    prefill_out = final[verify_count:]
    new_cache = jnp.stack([key_rows, value_rows], axis=2).reshape(all_rows.shape[0], -1)
    verify_cache = new_cache[:verify_count].reshape(req_count, draft_len, -1)
    keep_rows = jnp.arange(draft_len, dtype=jnp.int32)[None, :, None] < accepted[:, None, None]
    verify_kv = jnp.where(keep_rows, verify_cache, jnp.zeros_like(verify_cache))
    prefill_kv = new_cache[verify_count:]
    return (verify_out, prefill_out, verify_kv, prefill_kv)


def solution(mesh):
    placed = (
        P("req", None, None),
        P("req", None),
        P(),
        P(None, "head"),
        P(None, "head"),
        P(),
        P("head", None),
        P(),
        P("req", None, "head"),
        P("req", None),
        P("req", None),
        P("req"),
        P("req", None),
        P("req"),
    )
    return jax.shard_map(
        on_device,
        mesh=mesh,
        in_specs=placed,
        out_specs=(
            P("req", None, "head"),
            P("req", "head"),
            P("req", None, "head"),
            P("req", "head"),
        ),
        check_vma=False,
    )
```

profile of v0, /device:TPU:0, one launch (start us, length us, event | category | flops | bytes accessed | tf_op | source)
XLA Modules:
  0.0 95.3 jit_solution(530796960262207738)
XLA Ops:
  7.2 0.8 fusion.42
  8.0 0.7 compare_and_fusion
  9.4 1.8 %gather_fusion = bf16[16,16,512]{2,1,0:T(8,128)(2,1)S(1)} fusion(bf16[64,16,512]{2,1,0:T(8,128)(2,1)} %param.22, s32[1024]{0:T(1024)S(1)} %pad_clamp_fusion.1), kind=kCustom, calls=%fused_computation | custom fusion | bytes 524352 | tf_op jit(solution)/shard_map/jit(_take)/gather | solution.py:93
  11.3 0.8 select_select_fusion
  12.1 8.4 %all-to-all-start = ((bf16[16,16,512]{2,1,0:T(8,128)(2,1)}), bf16[16,16,512]{2,1,0:T(8,128)(2,1)}, u32[]{:S(2)}, u32[]{:S(2)}) async-start(bf16[16,16,512]{2,1,0:T(8,128)(2,1)} %select_select_fusion), calls=%async_computation | async-start | bytes 524288 | tf_op jit(solution)/shard_map/all_to_all | solution.py:95
  22.0 0.7 fusion.23
  24.5 1.6 %fusion.51 = f32[261,512]{1,0:T(8,128)} fusion(bf16[2048,512]{1,0:T(8,128)(2,1)S(1)} %copy-done, f32[2048]{0:T(1024)S(1)} %copy-done.22, f32[261]{0:T(512)S(1)} %add_rsqrt_fusion.4, bf16[256,2048]{1,0:T(8,128)(2,1)S(1)} %copy-done.2, bf16[5,2048]{1,0:T(8,128)(2,1)S(1)} %bitcast.115), kind=kOutput, calls=%fused_computation.125 | convolution fusion | flops 551098368 | bytes 3709972 | tf_op jit(solution)/shard_map/dot_general | solution.py:38
  26.1 2.2 %reshape.682 = f32[261,1,2,256]{3,2,0,1:T(2,128)} reshape(f32[261,512]{1,0:T(8,128)} %fusion.51) | data formatting | bytes 1069056 | tf_op jit(solution)/shard_map/reshape | solution.py:38
  28.3 1.7 %fusion.53 = (f32[261,1,1,256]{3,2,0,1:T(1,128)S(1)}, f32[261,1,1,256]{3,2,0,1:T(1,128)S(1)}) fusion(f32[261,1,2,256]{3,2,0,1:T(2,128)} %reshape.682), kind=kLoop, calls=%fused_computation.126 | loop fusion | bytes 1069056 | tf_op jit(solution)/shard_map/slice | solution.py:42
  30.5 1.3 %multiply_cosine_fusion = (f32[261,128]{1,0:T(8,128)}, f32[261,128]{1,0:T(8,128)}) fusion(f32[128]{0:T(128)S(1)} %multiply_power_fusion, f32[261]{0:T(512)S(1)} %pad_maximum_fusion.8), kind=kLoop, calls=%fused_computation.61 | loop fusion | flops 33408 | bytes 268820 | tf_op jit(solution)/shard_map/cos | solution.py:22
  31.7 1.2 %fusion.29 = (bf16[261,1,128]{2,0,1:T(8,128)(2,1)S(1)}, bf16[261,1,128]{2,0,1:T(8,128)(2,1)}) fusion(f32[261,1,256]{2,0,1:T(8,128)S(1)} %get-tuple-element.37, f32[128]{0:T(128)S(1)} %multiply_power_fusion, f32[261]{0:T(512)S(1)} %pad_maximum_fusion.8), kind=kLoop, calls=%fused_computation.71 | loop fusion | flops 300672 | bytes 402452 | tf_op jit(solution)/shard_map/convert.6
  34.3 4.6 %fusion.49 = f32[261,1024]{1,0:T(8,128)} fusion(bf16[2048,1024]{1,0:T(8,128)(2,1)} %param.17, f32[2048]{0:T(1024)S(1)} %copy-done.23, f32[261]{0:T(512)S(1)} %add_rsqrt_fusion.4, bf16[256,2048]{1,0:T(8,128)(2,1)S(1)} %copy-done.2, bf16[5,2048]{1,0:T(8,128)(2,1)S(1)} %bitcast.116), kind=kOutput, calls=%fused_computation.124 | convolution fusion | flops 1098455040 | bytes 6341652 | tf_op jit(solution)/shard_map/dot_general | solution.py:34
  38.9 1.8 %reshape.689 = f32[261,4,256]{2,1,0:T(4,128)S(1)} reshape(f32[261,1024]{1,0:T(8,128)} %fusion.49) | data formatting | bytes 2138112 | tf_op jit(solution)/shard_map/reshape | solution.py:34
  40.7 1.0 %multiply_reduce_fusion.1 = f32[261,4]{1,0:T(8,128)} fusion(f32[261,4,256]{2,1,0:T(4,128)S(1)} %reshape.689), kind=kLoop, calls=%fused_computation.23 | loop fusion | flops 533484 | bytes 1073232 | tf_op jit(solution)/shard_map/reduce_sum | solution.py:15
  41.7 1.0 %copy.55 = f32[261,4]{0,1:T(4,128)S(1)} copy(f32[261,4]{1,0:T(8,128)} %multiply_reduce_fusion.1) | data formatting | bytes 8352 | tf_op jit(solution)/shard_map/reduce_sum | solution.py:15
  42.7 0.7 maximum_bitcast_fusion.4
  43.5 0.9 fusion.8
  44.6 0.7 copy-done.5
  46.2 1.2 %convolution_convert_fusion = bf16[256,4,256]{2,0,1:T(8,128)(2,1)} fusion(f32[1,4,256,256]{2,3,1,0:T(8,128)S(1)} %get-tuple-element.33, f32[4,256]{1,0:T(4,128)S(1)} %fusion.9, f32[4,256]{1,0:T(4,128)S(1)} %get-tuple-element.32, bf16[261,1,256]{2,0,1:T(8,128)(2,1)S(1)} %copy-done.14), kind=kOutput, calls=%fused_computation.14 | convolution fusion | flops 135266304 | bytes 1712128 | tf_op jit(solution)/shard_map/gqtj,jge->tgqe/dot_general | solution.py:56
  47.6 2.1 %pad_maximum_fusion.1 = bf16[80,16,512]{2,1,0:T(8,128)(2,1)} fusion(bf16[16,16,512]{2,1,0:T(8,128)(2,1)} %all-to-all-done, bf16[64,16,512]{2,1,0:T(8,128)(2,1)S(1)} %copy-done.4), kind=kLoop, calls=%fused_computation.13 | loop fusion | flops 655360 | bytes 2621440 | tf_op jit(solution)/shard_map/concatenate | solution.py:96
  49.7 2.0 %gather_fusion.1 = bf16[64,16,512]{2,1,0:T(8,128)(2,1)S(1)} fusion(bf16[80,16,512]{2,1,0:T(8,128)(2,1)} %pad_maximum_fusion.1, s32[1024]{0:T(1024)} %pad_clamp_fusion), kind=kCustom, calls=%fused_computation.1 | custom fusion | bytes 2097408 | tf_op jit(solution)/shard_map/vmap(jit(_take))/gather | solution.py:112
  51.8 1.1 %gather.12 = bf16[1,1024,1,2,256]{4,3,1,2,0:T(2,128)(2,1)} reshape(bf16[64,16,512]{2,1,0:T(8,128)(2,1)S(1)} %gather_fusion.1) | data formatting | bytes 2097152 | tf_op jit(solution)/shard_map/vmap(jit(_take))/gather | solution.py:112
  52.9 1.4 %copy_select_fusion = bf16[1,1024,1,2,256]{4,1,3,2,0:T(8,128)(2,1)S(1)} fusion(bf16[1,1024,1,2,256]{4,3,1,2,0:T(2,128)(2,1)} %gather.12, pred[1024]{0:T(1024)(128)(4,1)S(1)} %broadcast_in_dim.141), kind=kLoop, calls=%fused_computation.24 | loop fusion | flops 524288 | bytes 2098176 | tf_op jit(solution)/shard_map/vmap(jit(_take))/select_n | solution.py:112
  54.4 0.8 copy-done.8
  56.4 5.1 %fusion.10 = f32[261,2048]{1,0:T(8,128)} fusion(bf16[1024,2048]{1,0:T(8,128)(2,1)} %param.20, bf16[256,1024]{0,1:T(8,128)(2,1)} %bitcast.123, bf16[5,1024]{0,1:T(8,128)(2,1)S(1)} %copy.59), kind=kOutput, calls=%fused_computation.29 | convolution fusion | flops 1095782400 | bytes 6866944 | tf_op jit(solution)/shard_map/dot_general | solution.py:139
  62.4 0.8 pad_maximum_fusion.4
  63.1 1.9 %copy.60 = bf16[256,1,2,256]{0,3,2,1:T(8,128)(2,1)} copy(bf16[256,1,2,256]{3,0,2,1:T(8,128)(2,1)} %pad_maximum_fusion.4) | data formatting | bytes 524288 | tf_op jit(solution)/shard_map/slice | solution.py:153
  65.0 1.8 %copy.61 = bf16[256,512]{1,0:T(8,128)(2,1)} copy(bf16[256,512]{0,1:T(8,128)(2,1)} %bitcast.113) | data formatting | bytes 524288
  66.8 0.7 broadcast_select_fusion
  67.5 16.7 %all-reduce.2.cloned.1.call-done = f32[261,2048]{1,0:T(8,128)} async-done(((f32[261,2048]{1,0:T(8,128)}), f32[261,2048]{1,0:T(8,128)}) %all-reduce.2.cloned.1.call-update) | async-done | bytes 2138128 | tf_op jit(solution)/shard_map/psum | solution.py:142
  84.2 2.0 %multiply_reduce_fusion = f32[261]{0:T(512)S(1)} fusion(f32[261,2048]{1,0:T(8,128)} %all-reduce.2.cloned.1.call-done), kind=kLoop, calls=%fused_computation.9 | loop fusion | flops 1068795 | bytes 2139156 | tf_op jit(solution)/shard_map/reduce_sum | solution.py:15
  87.5 0.9 slice.103
  (97 shorter events, 9.1 us)
Async XLA Ops:
  7.2 17.4 %copy-start = (bf16[2048,512]{1,0:T(8,128)(2,1)S(1)}, bf16[2048,512]{1,0:T(8,128)(2,1)}, u32[]{:S(2)}) copy-start(bf16[2048,512]{1,0:T(8,128)(2,1)} %param.18) | copy-start | bytes 6291460
  7.2 13.3 %copy-start.24 = (s32[1,64]{1,0:T(1,128)S(1)}, s32[1,64]{1,0:T(1,128)}, u32[]{:S(2)}) copy-start(s32[1,64]{1,0:T(1,128)} %param.24) | copy-start | bytes 772
  7.2 14.6 %copy-start.25 = (s32[1,4]{1,0:T(1,128)S(1)}, s32[1,4]{1,0:T(1,128)}, u32[]{:S(2)}) copy-start(s32[1,4]{1,0:T(1,128)} %param.26) | copy-start | bytes 52
  7.2 15.7 %copy-start.2 = (bf16[256,2048]{1,0:T(8,128)(2,1)S(1)}, bf16[256,2048]{1,0:T(8,128)(2,1)}, u32[]{:S(2)}) copy-start(bf16[256,2048]{1,0:T(8,128)(2,1)} %param.15) | copy-start | bytes 3145732
  7.2 15.7 %copy-start.15 = (bf16[1,5,2048]{2,1,0:T(8,128)(2,1)S(1)}, bf16[1,5,2048]{2,1,0:T(8,128)(2,1)}, u32[]{:S(2)}) copy-start(bf16[1,5,2048]{2,1,0:T(8,128)(2,1)} %param.14) | copy-start | bytes 61444
  9.4 13.9 %copy-start.20 = (f32[2,256]{1,0:T(2,128)S(1)}, f32[2,256]{1,0:T(2,128)}, u32[]{:S(2)}) copy-start(f32[2,256]{1,0:T(2,128)} %param.19) | copy-start | bytes 6148
  9.4 15.1 %copy-start.22 = (f32[2048]{0:T(1024)S(1)}, f32[2048]{0:T(1024)}, u32[]{:S(2)}) copy-start(f32[2048]{0:T(1024)} %param.16) | copy-start | bytes 24580
  12.1 35.5 %all-to-all-start = ((bf16[16,16,512]{2,1,0:T(8,128)(2,1)}), bf16[16,16,512]{2,1,0:T(8,128)(2,1)}, u32[]{:S(2)}, u32[]{:S(2)}) async-start(bf16[16,16,512]{2,1,0:T(8,128)(2,1)} %select_select_fusion), calls=%async_computation | async-start | bytes 524288 | tf_op jit(solution)/shard_map/all_to_all | solution.py:95
  20.4 63.8 %all-reduce.2.cloned.1.call-start = ((), (), s32[]{:S(2)}) async-start(), calls=%async_computation.1 | async-start | bytes 4325376 | tf_op jit(solution)/shard_map/psum | solution.py:142
  30.0 4.3 %copy-start.23 = (f32[2048]{0:T(1024)S(1)}, f32[2048]{0:T(1024)}, u32[]{:S(2)}) copy-start(f32[2048]{0:T(1024)} %param.16) | copy-start | bytes 24580
  30.4 3.9 %copy-start.17 = (f32[261]{0:T(512)}, f32[261]{0:T(512)S(1)}, u32[]{:S(2)}) copy-start(f32[261]{0:T(512)S(1)} %add_rsqrt_fusion.3) | copy-start | bytes 3136
  33.1 0.7 copy-start.13
  42.7 1.7 %copy-start.11 = (f32[261,128]{1,0:T(8,128)S(1)}, f32[261,128]{1,0:T(8,128)}, u32[]{:S(2)}) copy-start(f32[261,128]{1,0:T(8,128)} %get-tuple-element.28) | copy-start | bytes 400900
  42.7 1.7 %copy-start.12 = (f32[261,128]{1,0:T(8,128)S(1)}, f32[261,128]{1,0:T(8,128)}, u32[]{:S(2)}) copy-start(f32[261,128]{1,0:T(8,128)} %get-tuple-element.29) | copy-start | bytes 400900
  44.4 0.9 copy-start.5
  44.4 0.9 copy-start.16
  44.6 1.1 %copy-start.7 = (bf16[261,4,128]{2,0,1:T(8,128)(2,1)}, bf16[261,4,128]{2,0,1:T(8,128)(2,1)S(1)}, u32[]{:S(2)}) copy-start(bf16[261,4,128]{2,0,1:T(8,128)(2,1)S(1)} %get-tuple-element.20) | copy-start | bytes 801796
  44.6 1.1 %copy-start.9 = (bf16[261,4,128]{2,0,1:T(8,128)(2,1)}, bf16[261,4,128]{2,0,1:T(8,128)(2,1)S(1)}, u32[]{:S(2)}) copy-start(bf16[261,4,128]{2,0,1:T(8,128)(2,1)S(1)} %get-tuple-element.21) | copy-start | bytes 801796
  45.3 0.9 copy-start.14
  46.2 1.2 %copy-start.21 = (pred[64]{0:T(512)(128)(4,1)S(1)}, pred[64]{0:T(512)(128)(4,1)}, u32[]{:S(2)}) copy-start(pred[64]{0:T(512)(128)(4,1)} %and_bitcast_fusion) | copy-start | bytes 196
  46.2 1.4 %copy-start.4 = (bf16[64,16,512]{2,1,0:T(8,128)(2,1)S(1)}, bf16[64,16,512]{2,1,0:T(8,128)(2,1)}, u32[]{:S(2)}) copy-start(bf16[64,16,512]{2,1,0:T(8,128)(2,1)} %param.22) | copy-start | bytes 3145732
  54.3 1.0 %copy-start.8 = (bf16[261,4,128]{2,0,1:T(8,128)(2,1)S(1)}, bf16[261,4,128]{2,0,1:T(8,128)(2,1)}, u32[]{:S(2)}) copy-start(bf16[261,4,128]{2,0,1:T(8,128)(2,1)} %copy-done.7) | copy-start | bytes 801796
  54.3 1.0 %copy-start.10 = (bf16[261,4,128]{2,0,1:T(8,128)(2,1)S(1)}, bf16[261,4,128]{2,0,1:T(8,128)(2,1)}, u32[]{:S(2)}) copy-start(bf16[261,4,128]{2,0,1:T(8,128)(2,1)} %copy-done.9) | copy-start | bytes 801796
  54.4 1.6 %copy-start.19 = (bf16[1,5,1,256]{3,1,2,0:T(8,128)(2,1)S(1)}, bf16[1,5,1,256]{3,1,2,0:T(8,128)(2,1)}, u32[]{:S(2)}) copy-start(bf16[1,5,1,256]{3,1,2,0:T(8,128)(2,1)} %slice_bitcast_fusion.5) | copy-start | bytes 7684
  61.5 0.7 copy-start.18
  61.5 0.9 copy-start.6
  63.1 23.1 %copy-start.3 = (bf16[256,2048]{1,0:T(8,128)(2,1)S(1)}, bf16[256,2048]{1,0:T(8,128)(2,1)}, u32[]{:S(2)}) copy-start(bf16[256,2048]{1,0:T(8,128)(2,1)} %param.15) | copy-start | bytes 3145732
  66.8 19.4 %dynamic-slice-start = ((f32[2048]{0:T(1024)}, s32[]{:T(128)}), f32[1024]{0:T(1024)S(1)}, s32[]{:S(2)}) async-start(f32[2048]{0:T(1024)} %param.21, s32[]{:T(128)} %select_n.81), calls=%async_computation.2 | async-start | bytes 8704 | tf_op jit(solution)/shard_map/dynamic_slice | solution.py:145
  84.2 2.3 %copy-start.1 = (f32[261,2048]{1,0:T(8,128)S(1)}, f32[261,2048]{1,0:T(8,128)}, u32[]{:S(2)}) copy-start(f32[261,2048]{1,0:T(8,128)} %all-reduce.2.cloned.1.call-done) | copy-start | bytes 6414340
Sparse Core Ops, SparseCore 0:
  61.6 22.5 all-reduce.1
where the time goes:
time: 96.1 us; the launch traced here: 95.3 us
  local copies, waits for them, and re-layouts  21.4 us (22%)
  other arithmetic  19.6 us (20%)
  waiting for transfers between devices  16.7 us (17%)
  between operations  15.8 us (16%)
  matrix products  13.5 us (14%)
  starting transfers between devices  8.41 us (9%)
    psum x1, waiting for transfers between devices, on_device(): summed = lax.psum(partial_rows, 'head')  16.7 us
    all_to_all x1, starting transfers between devices, on_device(): lax.all_to_all(outgoing, 'req', split_axis=0, concat_axis=0, tiled=True)  8.36 us
    dot_general x1, matrix products, on_device(): partial_rows = jnp.dot(all_attn, w_out, preferred_element_type=jnp.float32)  5.1 us
    unnamed x53, local copies, waits for them, and re-layouts  4.78 us
    dot_general x1, matrix products, project(): jnp.dot(normed, w_query, preferred_element_type=jnp.float32)  4.62 us
    reduce_sum x5, other arithmetic, rms_scale(): jnp.mean(values * values, axis=-1, keepdims=True) + eps_norm  3.82 us
    gather x2, local copies, waits for them, and re-layouts, verify_one(): cached = jnp.take(pool_now, page_list, axis=0).reshape(-1, groups, 2, HEAD)  3.16 us
    reshape x1, local copies, waits for them, and re-layouts, project(): jnp.dot(normed, w_keyval, preferred_element_type=jnp.float32)  2.18 us
  transfers between devices with their start and end apart: 2, of which 1 were waited for; matrix products, arithmetic and copies ran while one was open for 31% of the time, Pallas kernels for 0%

commit v1 on v0

v1 whole, which is shorter than its diff:
```python
import functools

import jax
import jax.numpy as jnp
import numpy as np
from jax import lax
from jax.experimental import pallas as pl
from jax.experimental.pallas import tpu as pltpu
from jax.sharding import PartitionSpec as P

HEAD = 256
HALF = HEAD // 2
PAD = 16
SPAN = 256
eps_norm = 1e-06
rope_base = 1000000.0
neg_large = -1e30
MESH = pl.DeviceIdType.MESH


def rope_tables(longest):
    freq = rope_base ** (-2.0 * np.arange(HALF) / HEAD)
    low = np.arange(SPAN)[:, None] * freq[None, :]
    low = np.concatenate([np.cos(low), np.sin(low)], axis=1).astype(np.float32)
    coarse = low.astype(jnp.bfloat16)
    fine = (low - coarse.astype(np.float32)).astype(jnp.bfloat16)
    count = -(-(longest // SPAN + 1) // 8) * 8
    high = np.arange(count)[:, None] * float(SPAN) * freq[None, :]
    high = np.concatenate([np.cos(high), np.sin(high)], axis=1).astype(np.float32)
    return np.concatenate([coarse, fine], axis=1), high


def rms(values):
    return values * lax.rsqrt(jnp.mean(values * values, axis=-1, keepdims=True) + eps_norm)


def dot(a, b):
    return jnp.dot(a, b, preferred_element_type=jnp.float32)


def dot_t(a, b):
    return lax.dot_general(a, b, (((1,), (1,)), ((), ())), preferred_element_type=jnp.float32)


def kernel(
    n,
    outbound, page_table, cache_len, prompt_len, accepted,
    verify_x, prefill_x, attn_gain, w_query, w_keyval, qk_gain, w_out, post_gain,
    page_pool, table, high,
    verify_out, prefill_out, verify_kv, prefill_kv,
    x_v, vx_v, again_v, pgain_v, qkgain_v, table_v, high_v,
    wp_v, wo_v, pool_v, leaving, arrived, cached,
    normed, cos_v, sin_v, bias, kv_v, qv_v, attn_v, vattn_v,
    own_v, send_v, got_v, stat_v, gstat_v, vsend_v, vgot_v, out_v,
    local_sem, page_send, page_recv, ex_send, ex_recv,
):
    me = lax.axis_index("req")
    side = lax.axis_index("head")
    rows, width = x_v.shape
    draft = verify_x.shape[1]
    half = width // 2
    heads = attn_v.shape[1] // HEAD
    pages = page_table.shape[1]
    pool_pages = pool_v.shape[0]
    page_rows = pool_v.shape[1]
    mine = pl.multiple_of(side * half, half)
    theirs = pl.multiple_of((1 - side) * half, half)

    barrier = pltpu.get_barrier_semaphore()
    pl.semaphore_signal(barrier, inc=1, device_id=(me, 1 - side), device_id_type=MESH)

    def greet(step, carry):
        pl.semaphore_signal(
            barrier, inc=1, device_id=(lax.rem(me + step, n), side), device_id_type=MESH
        )
        return carry

    lax.fori_loop(1, n, greet, 0)

    copies = []

    def fetch(src, dst):
        copy = pltpu.make_async_copy(src, dst, local_sem.at[len(copies)])
        copy.start()
        copies.append(copy)
        return copy

    got_pool = fetch(page_pool, pool_v)
    got_x = fetch(prefill_x, x_v)
    got_again = fetch(attn_gain, again_v)
    got_w = [fetch(w_keyval.at[:, pl.ds(i * HEAD, HEAD)], wp_v.at[i]) for i in range(2)]
    got_table = fetch(table, table_v)
    got_high = fetch(high, high_v)
    got_qkgain = fetch(qk_gain, qkgain_v)
    got_w += [
        fetch(w_query.at[:, pl.ds(i * HEAD, HEAD)], wp_v.at[2 + i]) for i in range(heads)
    ]
    got_wo = [
        fetch(w_out.at[:, pl.ds(theirs, half)], wo_v.at[0]),
        fetch(w_out.at[:, pl.ds(mine, half)], wo_v.at[1]),
    ]
    got_pgain = fetch(post_gain, pgain_v)

    arrived[me] = jnp.zeros(arrived.shape[1:], arrived.dtype)
    got_pool.wait()

    def pack(d, carry):
        page = outbound[0, d]
        body = pool_v[jnp.clip(page, 0, pool_pages - 1)]
        leaving[d] = lax.select(page >= 0, body, jnp.zeros_like(body))
        return carry

    lax.fori_loop(0, n, pack, 0)

    vx_v[...] = jnp.zeros_like(vx_v)
    vx_v[0:draft, :] = verify_x[0].astype(jnp.float32)
    got_again.wait()
    normed[rows:, :] = (rms(vx_v[...]) * again_v[...]).astype(jnp.bfloat16)

    pl.semaphore_wait(barrier, n)

    def send(step, carry):
        d = lax.rem(me + step, n)
        pltpu.make_async_remote_copy(
            src_ref=leaving.at[d],
            dst_ref=arrived.at[me],
            send_sem=page_send.at[d],
            recv_sem=page_recv.at[me],
            device_id=(d, side),
            device_id_type=MESH,
        ).start()
        return carry

    lax.fori_loop(1, n, send, 0)

    got_x.wait()
    block = 32

    def norm_rows(i, carry):
        at = pl.ds(pl.multiple_of(i * block, block), block)
        normed[at, :] = (rms(x_v[at, :].astype(jnp.float32)) * again_v[...]).astype(jnp.bfloat16)
        return carry

    lax.fori_loop(0, rows // block, norm_rows, 0)

    row = lax.broadcasted_iota(jnp.int32, (rows, 1), 0)
    start = jnp.zeros((rows, 1), jnp.int32)
    end = jnp.int32(0)
    for k in range(prompt_len.shape[1] - 1):
        end = end + prompt_len[0, k]
        start = jnp.where(row >= end, end, start)
    col = lax.broadcasted_iota(jnp.int32, (rows, rows), 1)
    bias[...] = jnp.where((col <= row) & (col >= start), 0.0, neg_large)
    length = cache_len[0]
    vrow = lax.broadcasted_iota(jnp.int32, (PAD, 1), 0)
    vpos = length + jnp.minimum(vrow, draft - 1)
    lane = lax.broadcasted_iota(jnp.int32, (rows, SPAN), 1)
    vlane = lax.broadcasted_iota(jnp.int32, (PAD, SPAN), 1)
    got_table.wait()
    got_high.wait()
    got_qkgain.wait()

    def factors(pick):
        both = dot(jnp.where(pick, 1.0, 0.0).astype(jnp.bfloat16), table_v[...])
        return (
            both[:, :HALF] + both[:, HEAD:HEAD + HALF],
            both[:, HALF:HEAD] + both[:, HEAD + HALF:],
        )

    cos_p, sin_p = factors(lane == row - start)
    cos_v[0:rows, :] = cos_p
    sin_v[0:rows, :] = sin_p
    cos_l, sin_l = factors(vlane == jnp.bitwise_and(vpos, SPAN - 1))
    far = lax.shift_right_logical(vpos, 8)
    cos_h = jnp.zeros((PAD, HALF), jnp.float32)
    sin_h = jnp.zeros((PAD, HALF), jnp.float32)
    for k in range(high_v.shape[0]):
        cos_h = jnp.where(far == k, high_v[k:k + 1, :HALF], cos_h)
        sin_h = jnp.where(far == k, high_v[k:k + 1, HALF:], sin_h)
    cos_v[rows:, :] = cos_l * cos_h - sin_l * sin_h
    sin_v[rows:, :] = sin_l * cos_h + cos_l * sin_h

    def rope(values):
        first, second = values[:, :HALF], values[:, HALF:]
        cosine, sine = cos_v[...], sin_v[...]
        return jnp.concatenate(
            [first * cosine - second * sine, second * cosine + first * sine], axis=-1
        ).astype(jnp.bfloat16)

    got_w[0].wait()
    kv_v[:, :HEAD] = rope(rms(dot(normed[...], wp_v[0])) * qkgain_v[1:2, :])
    got_w[1].wait()
    kv_v[:, HEAD:] = rms(dot(normed[...], wp_v[1])).astype(jnp.bfloat16)
    put_kv = pltpu.make_async_copy(
        kv_v.at[pl.ds(0, rows)], prefill_kv, local_sem.at[len(copies)]
    )
    put_kv.start()
    vkv = kv_v[rows:, :].astype(jnp.float32)
    vkv = jnp.where(vrow < accepted[0], vkv, 0.0).astype(jnp.bfloat16)
    verify_kv[0] = vkv[0:draft, :]

    for i in range(heads):
        got_w[2 + i].wait()
        query = rope(rms(dot(normed[...], wp_v[2 + i])) * qkgain_v[0:1, :])
        qv_v[i * PAD:(i + 1) * PAD, :] = query[rows:, :]
        scores = dot_t(query[:rows, :], kv_v[:rows, :HEAD]) + bias[...]
        weights = jnp.exp(scores - jnp.max(scores, axis=-1, keepdims=True))
        probs = (weights / jnp.sum(weights, axis=-1, keepdims=True)).astype(jnp.bfloat16)
        attn_v[:, i * HEAD:(i + 1) * HEAD] = dot(probs, kv_v[:rows, HEAD:]).astype(jnp.bfloat16)

    def swap(src, dst, k):
        copy = pltpu.make_async_remote_copy(
            src_ref=src,
            dst_ref=dst,
            send_sem=ex_send.at[k],
            recv_sem=ex_recv.at[k],
            device_id=(me, 1 - side),
            device_id_type=MESH,
        )
        copy.start()
        return copy

    got_wo[0].wait()
    send_v[...] = dot(attn_v[...], wo_v[0]).astype(send_v.dtype)
    swap_rows = swap(send_v, got_v, 0)
    got_wo[1].wait()
    own_v[...] = dot(attn_v[...], wo_v[1])

    def arrive(step, carry):
        s = lax.rem(me + n - step, n)
        pltpu.make_async_remote_copy(
            src_ref=leaving.at[s],
            dst_ref=arrived.at[s],
            send_sem=page_send.at[s],
            recv_sem=page_recv.at[s],
            device_id=(s, side),
            device_id_type=MESH,
        ).wait()
        return carry

    lax.fori_loop(1, n, arrive, 0)

    def gather(i, carry):
        page = page_table[0, i]
        local = pool_v[jnp.minimum(page, pool_pages - 1)]
        moved = arrived[jnp.clip(page - pool_pages, 0, n - 1)]
        at = pl.ds(pl.multiple_of(i * page_rows, page_rows), page_rows)
        cached[at, :] = lax.select(page < pool_pages, local, moved)
        return carry

    lax.fori_loop(0, pages, gather, 0)

    queries = qv_v[...]
    old = dot_t(queries, cached[:, :HEAD])
    slot = lax.broadcasted_iota(jnp.int32, old.shape, 1)
    old = jnp.where(slot < length, old, neg_large)
    new = dot_t(queries, kv_v[rows:, :HEAD])
    step = jnp.bitwise_and(lax.broadcasted_iota(jnp.int32, new.shape, 0), PAD - 1)
    new = jnp.where(lax.broadcasted_iota(jnp.int32, new.shape, 1) <= step, new, neg_large)
    peak = jnp.maximum(
        jnp.max(old, axis=-1, keepdims=True), jnp.max(new, axis=-1, keepdims=True)
    )
    old = jnp.exp(old - peak)
    new = jnp.exp(new - peak)
    total = jnp.sum(old, axis=-1, keepdims=True) + jnp.sum(new, axis=-1, keepdims=True)
    mixed = dot((old / total).astype(jnp.bfloat16), cached[:, HEAD:])
    mixed = mixed + dot((new / total).astype(jnp.bfloat16), kv_v[rows:, HEAD:])
    mixed = mixed.astype(jnp.bfloat16)
    for i in range(heads):
        vattn_v[:, i * HEAD:(i + 1) * HEAD] = mixed[i * PAD:(i + 1) * PAD, :]

    swap_rows.wait()
    summed = own_v[...] + got_v[...].astype(jnp.float32)
    own_v[...] = summed
    stat_v[...] = jnp.broadcast_to(jnp.sum(summed * summed, axis=-1, keepdims=True), stat_v.shape)
    swap_stat = swap(stat_v, gstat_v, 1)

    vsend_v[0] = dot(vattn_v[...], wo_v[0])
    vsend_v[1] = dot(vattn_v[...], wo_v[1])
    swap_verify = swap(vsend_v, vgot_v, 2)

    got_pgain.wait()
    gain = pgain_v[:, pl.ds(mine, half)]
    swap_stat.wait()
    square = stat_v[:, 0:1] + gstat_v[:, 0:1]
    scale = lax.rsqrt(square / width + eps_norm)
    out_v[...] = (
        x_v[:, pl.ds(mine, half)].astype(jnp.float32) + own_v[...] * scale * gain
    ).astype(out_v.dtype)
    put_out = pltpu.make_async_copy(out_v, prefill_out, local_sem.at[len(copies) + 1])
    put_out.start()

    swap_verify.wait()
    ours = vsend_v[1] + vgot_v[0]
    other = vsend_v[0] + vgot_v[1]
    square = jnp.sum(ours * ours, axis=-1, keepdims=True)
    square = square + jnp.sum(other * other, axis=-1, keepdims=True)
    final = vx_v[:, pl.ds(mine, half)] + ours * lax.rsqrt(square / width + eps_norm) * gain
    verify_out[0] = final[0:draft, :].astype(verify_out.dtype)
    put_kv.wait()
    put_out.wait()


def on_device(
    verify_x, prefill_x, attn_gain, w_query, w_keyval, qk_gain, w_out, post_gain,
    page_pool, outbound, page_table, cache_len, prompt_len, accepted,
):
    n = lax.axis_size("req")
    _, draft, width = verify_x.shape
    rows = prefill_x.shape[0]
    all_rows = rows + PAD
    columns = w_query.shape[1]
    heads = columns // HEAD
    half = width // 2
    pages = page_table.shape[1]
    page = page_pool.shape[1:]
    table, high = rope_tables(pages * page[0] + draft)
    bf16, f32 = jnp.bfloat16, jnp.float32
    smem = pl.BlockSpec(memory_space=pltpu.SMEM)
    vmem = pl.BlockSpec(memory_space=pltpu.VMEM)
    hbm = pl.BlockSpec(memory_space=pl.ANY)
    fetched = 14 + heads
    return pl.pallas_call(
        functools.partial(kernel, n),
        out_shape=(
            jax.ShapeDtypeStruct((1, draft, half), bf16),
            jax.ShapeDtypeStruct((rows, half), bf16),
            jax.ShapeDtypeStruct((1, draft, 2 * HEAD), bf16),
            jax.ShapeDtypeStruct((rows, 2 * HEAD), bf16),
        ),
        in_specs=[smem] * 5 + [vmem] + [hbm] * 10,
        out_specs=(vmem, hbm, vmem, hbm),
        scratch_shapes=[
            pltpu.VMEM((rows, width), bf16),
            pltpu.VMEM((PAD, width), f32),
            pltpu.VMEM((1, width), f32),
            pltpu.VMEM((1, width), f32),
            pltpu.VMEM(qk_gain.shape, f32),
            pltpu.VMEM(table.shape, bf16),
            pltpu.VMEM(high.shape, f32),
            pltpu.VMEM((2 + heads, width, HEAD), bf16),
            pltpu.VMEM((2, columns, half), bf16),
            pltpu.VMEM(page_pool.shape, bf16),
            pltpu.VMEM((n,) + page, bf16),
            pltpu.VMEM((n,) + page, bf16),
            pltpu.VMEM((pages * page[0], page[1]), bf16),
            pltpu.VMEM((all_rows, width), bf16),
            pltpu.VMEM((all_rows, HALF), f32),
            pltpu.VMEM((all_rows, HALF), f32),
            pltpu.VMEM((rows, rows), f32),
            pltpu.VMEM((all_rows, 2 * HEAD), bf16),
            pltpu.VMEM((heads * PAD, HEAD), bf16),
            pltpu.VMEM((rows, columns), bf16),
            pltpu.VMEM((PAD, columns), bf16),
            pltpu.VMEM((rows, half), f32),
            pltpu.VMEM((rows, half), bf16),
            pltpu.VMEM((rows, half), bf16),
            pltpu.VMEM((rows, 128), f32),
            pltpu.VMEM((rows, 128), f32),
            pltpu.VMEM((2, PAD, half), f32),
            pltpu.VMEM((2, PAD, half), f32),
            pltpu.VMEM((rows, half), bf16),
            pltpu.SemaphoreType.DMA((fetched,)),
            pltpu.SemaphoreType.DMA((n,)),
            pltpu.SemaphoreType.DMA((n,)),
            pltpu.SemaphoreType.DMA((3,)),
            pltpu.SemaphoreType.DMA((3,)),
        ],
        compiler_params=pltpu.CompilerParams(
            collective_id=0, has_side_effects=True, vmem_limit_bytes=48 * 1024 * 1024
        ),
        cost_estimate=pl.CostEstimate(
            flops=2 * all_rows * width * (2 * columns + 2 * HEAD),
            bytes_accessed=16 * 1024 * 1024,
            transcendentals=heads * rows * rows,
        ),
    )(
        outbound, page_table, cache_len, prompt_len, accepted,
        verify_x, prefill_x, attn_gain.reshape(1, -1), w_query, w_keyval, qk_gain, w_out,
        post_gain.reshape(1, -1), page_pool, jnp.asarray(table), jnp.asarray(high),
    )


def solution(mesh):
    placed = (
        P("req", None, None),
        P("req", None),
        P(),
        P(None, "head"),
        P(None, "head"),
        P(),
        P("head", None),
        P(),
        P("req", None, "head"),
        P("req", None),
        P("req", None),
        P("req"),
        P("req", None),
        P("req"),
    )
    return jax.shard_map(
        on_device,
        mesh=mesh,
        in_specs=placed,
        out_specs=(
            P("req", None, "head"),
            P("req", "head"),
            P("req", None, "head"),
            P("req", "head"),
        ),
        check_vma=False,
    )
```

time: 96.1 us -> 36.7 us (0.38)
  Pallas kernels: 0 us -> 21 us
  other arithmetic: 19.6 us -> 0 us
  waiting for transfers between devices: 16.7 us -> 0 us
  between operations: 15.8 us -> 1.96 us
  matrix products: 13.5 us -> 0 us
  starting transfers between devices: 8.41 us -> 0 us
  local copies, waits for them, and re-layouts: 21.4 us -> 13.2 us
    pallas_call x0 -> x1, Pallas kernels: none -> 21 us  [on_device(): pl.pallas_call(functools.partial(kernel, n), out_shape=(jax.ShapeDtypeStr...]
    psum x1 -> x0, waiting for transfers between devices: 16.7 us -> none  [on_device(): summed = lax.psum(partial_rows, 'head')]
    dot_general x7 -> x0, matrix products: 13.5 us -> none  [the longest x1 5.1 us: on_device(): partial_rows = jnp.dot(all_attn, w_out, preferred_element_type=jnp.float32)]
    unnamed x53 -> x28, local copies, waits for them, and re-layouts: 4.78 us -> 13.2 us
    all_to_all x1 -> x0, starting transfers between devices: 8.36 us -> none  [on_device(): lax.all_to_all(outgoing, 'req', split_axis=0, concat_axis=0, tiled=True)]
    reshape x4 -> x0, local copies, waits for them, and re-layouts: 5.14 us -> none  [the longest x1 2.18 us: project(): jnp.dot(normed, w_keyval, preferred_element_type=jnp.float32)]
    slice x4 -> x0, local copies, waits for them, and re-layouts: 5.07 us -> none  [the longest x1 1.88 us: on_device(): prefill_kv = new_cache[verify_count:]]
    gather x3 -> x0, local copies, waits for them, and re-layouts: 4.96 us -> none  [the longest x2 3.16 us: verify_one(): cached = jnp.take(pool_now, page_list, axis=0).reshape(-1, groups, 2, HEAD)]
  transfers between devices with their start and end apart: 2 -> 0, of which waited for: 1 -> 0; matrix products, arithmetic and copies ran while one was open for 31% -> 0% of each run, Pallas kernels for 0% -> 0%
where the time goes in v1:
time: 36.7 us; the launch traced here: 36.1 us
  Pallas kernels  21 us (57%)
  local copies, waits for them, and re-layouts  13.2 us (36%)
  between operations  1.96 us (5%)
    pallas_call x1, Pallas kernels, on_device(): pl.pallas_call(functools.partial(kernel, n), out_shape=(jax.ShapeDtypeStr...  21 us
    unnamed x28, local copies, waits for them, and re-layouts  13.2 us

profile of v1, /device:TPU:0, one launch (start us, length us, event | category | flops | bytes accessed | tf_op | source)
XLA Modules:
  0.0 36.1 jit_solution(12234279586684636794)
XLA Ops:
  1.9 0.0 copy-start
  1.9 1.6 %copy-done = bf16[2048,512]{1,0:T(8,128)(2,1)S(1)} copy-done((bf16[2048,512]{1,0:T(8,128)(2,1)S(1)}, bf16[2048,512]{1,0:T(8,128)(2,1)}, u32[]{:S(2)}) %copy-start) | copy-done | bytes 2097176
  3.5 0.0 copy-start.1
  3.5 1.2 %copy-done.1 = bf16[256,2048]{1,0:T(8,128)(2,1)S(1)} copy-done((bf16[256,2048]{1,0:T(8,128)(2,1)S(1)}, bf16[256,2048]{1,0:T(8,128)(2,1)}, u32[]{:S(2)}) %copy-start.1) | copy-done | bytes 1048600
  4.7 0.0 copy-start.2
  4.7 1.2 %copy-done.2 = bf16[64,16,512]{2,1,0:T(8,128)(2,1)S(1)} copy-done((bf16[64,16,512]{2,1,0:T(8,128)(2,1)S(1)}, bf16[64,16,512]{2,1,0:T(8,128)(2,1)}, u32[]{:S(2)}) %copy-start.2) | copy-done | bytes 1048600
  6.0 0.0 copy-start.3
  6.0 0.9 %copy-done.3 = bf16[256,512]{1,0:T(8,128)(2,1)S(1)} copy-done((bf16[256,512]{1,0:T(8,128)(2,1)S(1)}, bf16[256,512]{1,0:T(8,128)(2,1)}, u32[]{:S(2)}) %copy-start.3) | copy-done | bytes 262168
  6.9 0.0 copy-start.4
  6.9 0.8 %copy-done.4 = bf16[1,5,2048]{2,1,0:T(8,128)(2,1)S(1)} copy-done((bf16[1,5,2048]{2,1,0:T(8,128)(2,1)S(1)}, bf16[1,5,2048]{2,1,0:T(8,128)(2,1)}, u32[]{:S(2)}) %copy-start.4) | copy-done | bytes 20504
  7.7 0.0 copy-start.5
  7.7 0.7 %copy-done.5 = f32[2048]{0:T(1024)S(1)} copy-done((f32[2048]{0:T(1024)S(1)}, f32[2048]{0:T(1024)}, u32[]{:S(2)}) %copy-start.5) | copy-done | bytes 8216
  8.4 0.0 copy-start.6
  8.4 0.7 %copy-done.6 = f32[2048]{0:T(1024)S(1)} copy-done((f32[2048]{0:T(1024)S(1)}, f32[2048]{0:T(1024)}, u32[]{:S(2)}) %copy-start.6) | copy-done | bytes 8216
  9.1 0.0 copy-start.7
  9.1 0.7 %copy-done.7 = f32[8,256]{1,0:T(8,128)S(1)} copy-done((f32[8,256]{1,0:T(8,128)S(1)}, f32[8,256]{1,0:T(8,128)}, u32[]{:S(2)}) %copy-start.7) | copy-done | bytes 8216
  9.8 0.0 copy-start.8
  9.8 0.7 %copy-done.8 = f32[2,256]{1,0:T(2,128)S(1)} copy-done((f32[2,256]{1,0:T(2,128)S(1)}, f32[2,256]{1,0:T(2,128)}, u32[]{:S(2)}) %copy-start.8) | copy-done | bytes 2072
  10.5 0.0 copy-start.9
  10.5 0.7 %copy-done.9 = s32[1,16]{1,0:T(1,128)S(1)} copy-done((s32[1,16]{1,0:T(1,128)S(1)}, s32[1,16]{1,0:T(1,128)}, u32[]{:S(2)}) %copy-start.9) | copy-done | bytes 88
  11.1 0.0 copy-start.10
  11.1 0.7 %copy-done.10 = s32[1,64]{1,0:T(1,128)S(1)} copy-done((s32[1,64]{1,0:T(1,128)S(1)}, s32[1,64]{1,0:T(1,128)}, u32[]{:S(2)}) %copy-start.10) | copy-done | bytes 280
  11.8 0.0 copy-start.11
  11.8 0.7 %copy-done.11 = s32[1,4]{1,0:T(1,128)S(1)} copy-done((s32[1,4]{1,0:T(1,128)S(1)}, s32[1,4]{1,0:T(1,128)}, u32[]{:S(2)}) %copy-start.11) | copy-done | bytes 40
  12.4 21.0 %shard_map.183 = (bf16[1,5,1024]{2,1,0:T(8,128)(2,1)S(1)}, bf16[256,1024]{1,0:T(8,128)(2,1)S(1)}, bf16[1,5,512]{2,1,0:T(8,128)(2,1)S(1)}, bf16[256,512]{1,0:T(8,128)(2,1)S(1)}) custom-call(s32[1,16]{1,0:T(1,128)S(1)} %copy-done.9, s32[1,64]{1,0:T(1,128)S(1)} %copy-done.10, s32[1]{0:T(128)S(6)} %copy.24.cache_len, s32[1,4]{1,0:T(1,128)S(1)} %copy-done.11, ...), custom_call_target="tpu_custom_call" | custom-call | flops 2852126720 | bytes 16777216 | tf_op jit(solution)/shard_map/pallas_call | solution.py:323
  33.4 0.6 %copy.26 = bf16[1,5,1024]{2,1,0:T(8,128)(2,1)} copy(bf16[1,5,1024]{2,1,0:T(8,128)(2,1)S(1)} %get-tuple-element.8) | data formatting | bytes 20480
  34.0 0.8 %copy.27 = bf16[256,1024]{1,0:T(8,128)(2,1)} copy(bf16[256,1024]{1,0:T(8,128)(2,1)S(1)} %get-tuple-element.9) | data formatting | bytes 1048576
  34.8 0.6 %copy.28 = bf16[1,5,512]{2,1,0:T(8,128)(2,1)} copy(bf16[1,5,512]{2,1,0:T(8,128)(2,1)S(1)} %get-tuple-element.10) | data formatting | bytes 10240
  35.4 0.7 %copy.29 = bf16[256,512]{1,0:T(8,128)(2,1)} copy(bf16[256,512]{1,0:T(8,128)(2,1)S(1)} %get-tuple-element.11) | data formatting | bytes 524288
Async XLA Ops:
  1.9 1.6 %copy-start = (bf16[2048,512]{1,0:T(8,128)(2,1)S(1)}, bf16[2048,512]{1,0:T(8,128)(2,1)}, u32[]{:S(2)}) copy-start(bf16[2048,512]{1,0:T(8,128)(2,1)} %w_keyval.1) | copy-start | bytes 6291460
  3.5 1.2 %copy-start.1 = (bf16[256,2048]{1,0:T(8,128)(2,1)S(1)}, bf16[256,2048]{1,0:T(8,128)(2,1)}, u32[]{:S(2)}) copy-start(bf16[256,2048]{1,0:T(8,128)(2,1)} %prefill_x.1) | copy-start | bytes 3145732
  4.7 1.2 %copy-start.2 = (bf16[64,16,512]{2,1,0:T(8,128)(2,1)S(1)}, bf16[64,16,512]{2,1,0:T(8,128)(2,1)}, u32[]{:S(2)}) copy-start(bf16[64,16,512]{2,1,0:T(8,128)(2,1)} %page_pool.1) | copy-start | bytes 3145732
  6.0 0.9 %copy-start.3 = (bf16[256,512]{1,0:T(8,128)(2,1)S(1)}, bf16[256,512]{1,0:T(8,128)(2,1)}, u32[]{:S(2)}) copy-start(bf16[256,512]{1,0:T(8,128)(2,1)} %constant.4.clone.table) | copy-start | bytes 786436
  6.9 0.8 %copy-start.4 = (bf16[1,5,2048]{2,1,0:T(8,128)(2,1)S(1)}, bf16[1,5,2048]{2,1,0:T(8,128)(2,1)}, u32[]{:S(2)}) copy-start(bf16[1,5,2048]{2,1,0:T(8,128)(2,1)} %verify_x.1) | copy-start | bytes 61444
  7.7 0.7 %copy-start.5 = (f32[2048]{0:T(1024)S(1)}, f32[2048]{0:T(1024)}, u32[]{:S(2)}) copy-start(f32[2048]{0:T(1024)} %param.18) | copy-start | bytes 24580
  8.4 0.7 %copy-start.6 = (f32[2048]{0:T(1024)S(1)}, f32[2048]{0:T(1024)}, u32[]{:S(2)}) copy-start(f32[2048]{0:T(1024)} %param.23) | copy-start | bytes 24580
  9.1 0.7 %copy-start.7 = (f32[8,256]{1,0:T(8,128)S(1)}, f32[8,256]{1,0:T(8,128)}, u32[]{:S(2)}) copy-start(f32[8,256]{1,0:T(8,128)} %constant.5.clone.high) | copy-start | bytes 24580
  9.8 0.7 %copy-start.8 = (f32[2,256]{1,0:T(2,128)S(1)}, f32[2,256]{1,0:T(2,128)}, u32[]{:S(2)}) copy-start(f32[2,256]{1,0:T(2,128)} %qk_gain.1) | copy-start | bytes 6148
  10.5 0.7 %copy-start.9 = (s32[1,16]{1,0:T(1,128)S(1)}, s32[1,16]{1,0:T(1,128)}, u32[]{:S(2)}) copy-start(s32[1,16]{1,0:T(1,128)} %outbound.1) | copy-start | bytes 196
  11.1 0.7 %copy-start.10 = (s32[1,64]{1,0:T(1,128)S(1)}, s32[1,64]{1,0:T(1,128)}, u32[]{:S(2)}) copy-start(s32[1,64]{1,0:T(1,128)} %page_table.1) | copy-start | bytes 772
  11.8 0.7 %copy-start.11 = (s32[1,4]{1,0:T(1,128)S(1)}, s32[1,4]{1,0:T(1,128)}, u32[]{:S(2)}) copy-start(s32[1,4]{1,0:T(1,128)} %prompt_len.1) | copy-start | bytes 52

commit v2 on v1

--- a/solution.py
+++ b/solution.py
@@ -10,6 +10,7 @@
 
 HEAD = 256
 HALF = HEAD // 2
+VMEM_LIMIT = 62 * 1024 * 1024
 PAD = 16
 SPAN = 256
 eps_norm = 1e-06
@@ -44,14 +45,15 @@
 
 def kernel(
     n,
-    outbound, page_table, cache_len, prompt_len, accepted,
-    verify_x, prefill_x, attn_gain, w_query, w_keyval, qk_gain, w_out, post_gain,
+    outbound_h, page_table_h, cache_len_h, prompt_len_h, accepted_h,
+    verify_h, prefill_x, attn_gain, w_query, w_keyval, qk_gain, w_out, post_gain,
     page_pool, table, high,
     verify_out, prefill_out, verify_kv, prefill_kv,
+    outbound, page_table, cache_len, prompt_len, accepted, verify_x,
     x_v, vx_v, again_v, pgain_v, qkgain_v, table_v, high_v,
     wp_v, wo_v, pool_v, leaving, arrived, cached,
     normed, cos_v, sin_v, bias, kv_v, qv_v, attn_v, vattn_v,
-    own_v, send_v, got_v, stat_v, gstat_v, vsend_v, vgot_v, out_v,
+    own_v, send_v, got_v, stat_v, gstat_v, vsend_v, vgot_v, out_v, vout_v, vkv_v,
     local_sem, page_send, page_recv, ex_send, ex_recv,
 ):
     me = lax.axis_index("req")
@@ -85,9 +87,18 @@
         copies.append(copy)
         return copy
 
+    put = fetch
+    got_outbound = fetch(outbound_h, outbound)
     got_pool = fetch(page_pool, pool_v)
+    got_verify = fetch(verify_h, verify_x)
+    got_again = fetch(attn_gain, again_v)
     got_x = fetch(prefill_x, x_v)
-    got_again = fetch(attn_gain, again_v)
+    got_small = [
+        fetch(prompt_len_h, prompt_len),
+        fetch(cache_len_h, cache_len),
+        fetch(accepted_h, accepted),
+        fetch(page_table_h, page_table),
+    ]
     got_w = [fetch(w_keyval.at[:, pl.ds(i * HEAD, HEAD)], wp_v.at[i]) for i in range(2)]
     got_table = fetch(table, table_v)
     got_high = fetch(high, high_v)
@@ -102,6 +113,7 @@
     got_pgain = fetch(post_gain, pgain_v)
 
     arrived[me] = jnp.zeros(arrived.shape[1:], arrived.dtype)
+    got_outbound.wait()
     got_pool.wait()
 
     def pack(d, carry):
@@ -113,8 +125,9 @@
     lax.fori_loop(0, n, pack, 0)
 
     vx_v[...] = jnp.zeros_like(vx_v)
+    got_verify.wait()
+    got_again.wait()
     vx_v[0:draft, :] = verify_x[0].astype(jnp.float32)
-    got_again.wait()
     normed[rows:, :] = (rms(vx_v[...]) * again_v[...]).astype(jnp.bfloat16)
 
     pl.semaphore_wait(barrier, n)
@@ -143,6 +156,8 @@
 
     lax.fori_loop(0, rows // block, norm_rows, 0)
 
+    for copy in got_small:
+        copy.wait()
     row = lax.broadcasted_iota(jnp.int32, (rows, 1), 0)
     start = jnp.zeros((rows, 1), jnp.int32)
     end = jnp.int32(0)
@@ -151,7 +166,7 @@
         start = jnp.where(row >= end, end, start)
     col = lax.broadcasted_iota(jnp.int32, (rows, rows), 1)
     bias[...] = jnp.where((col <= row) & (col >= start), 0.0, neg_large)
-    length = cache_len[0]
+    length = cache_len[0, 0]
     vrow = lax.broadcasted_iota(jnp.int32, (PAD, 1), 0)
     vpos = length + jnp.minimum(vrow, draft - 1)
     lane = lax.broadcasted_iota(jnp.int32, (rows, SPAN), 1)
@@ -191,13 +206,11 @@
     kv_v[:, :HEAD] = rope(rms(dot(normed[...], wp_v[0])) * qkgain_v[1:2, :])
     got_w[1].wait()
     kv_v[:, HEAD:] = rms(dot(normed[...], wp_v[1])).astype(jnp.bfloat16)
-    put_kv = pltpu.make_async_copy(
-        kv_v.at[pl.ds(0, rows)], prefill_kv, local_sem.at[len(copies)]
-    )
-    put_kv.start()
+    put_kv = put(kv_v.at[pl.ds(0, rows)], prefill_kv)
     vkv = kv_v[rows:, :].astype(jnp.float32)
-    vkv = jnp.where(vrow < accepted[0], vkv, 0.0).astype(jnp.bfloat16)
-    verify_kv[0] = vkv[0:draft, :]
+    vkv = jnp.where(vrow < accepted[0, 0], vkv, 0.0).astype(jnp.bfloat16)
+    vkv_v[0] = vkv[0:draft, :]
+    put_vkv = put(vkv_v, verify_kv)
 
     for i in range(heads):
         got_w[2 + i].wait()
@@ -205,7 +218,8 @@
         qv_v[i * PAD:(i + 1) * PAD, :] = query[rows:, :]
         scores = dot_t(query[:rows, :], kv_v[:rows, :HEAD]) + bias[...]
         weights = jnp.exp(scores - jnp.max(scores, axis=-1, keepdims=True))
-        probs = (weights / jnp.sum(weights, axis=-1, keepdims=True)).astype(jnp.bfloat16)
+        share = 1.0 / jnp.sum(weights, axis=-1, keepdims=True)
+        probs = (weights * share).astype(jnp.bfloat16)
         attn_v[:, i * HEAD:(i + 1) * HEAD] = dot(probs, kv_v[:rows, HEAD:]).astype(jnp.bfloat16)
 
     def swap(src, dst, k):
@@ -262,9 +276,9 @@
     )
     old = jnp.exp(old - peak)
     new = jnp.exp(new - peak)
-    total = jnp.sum(old, axis=-1, keepdims=True) + jnp.sum(new, axis=-1, keepdims=True)
-    mixed = dot((old / total).astype(jnp.bfloat16), cached[:, HEAD:])
-    mixed = mixed + dot((new / total).astype(jnp.bfloat16), kv_v[rows:, HEAD:])
+    share = 1.0 / (jnp.sum(old, axis=-1, keepdims=True) + jnp.sum(new, axis=-1, keepdims=True))
+    mixed = dot((old * share).astype(jnp.bfloat16), cached[:, HEAD:])
+    mixed = mixed + dot((new * share).astype(jnp.bfloat16), kv_v[rows:, HEAD:])
     mixed = mixed.astype(jnp.bfloat16)
     for i in range(heads):
         vattn_v[:, i * HEAD:(i + 1) * HEAD] = mixed[i * PAD:(i + 1) * PAD, :]
@@ -287,8 +301,7 @@
     out_v[...] = (
         x_v[:, pl.ds(mine, half)].astype(jnp.float32) + own_v[...] * scale * gain
     ).astype(out_v.dtype)
-    put_out = pltpu.make_async_copy(out_v, prefill_out, local_sem.at[len(copies) + 1])
-    put_out.start()
+    put_out = put(out_v, prefill_out)
 
     swap_verify.wait()
     ours = vsend_v[1] + vgot_v[0]
@@ -296,9 +309,22 @@
     square = jnp.sum(ours * ours, axis=-1, keepdims=True)
     square = square + jnp.sum(other * other, axis=-1, keepdims=True)
     final = vx_v[:, pl.ds(mine, half)] + ours * lax.rsqrt(square / width + eps_norm) * gain
-    verify_out[0] = final[0:draft, :].astype(verify_out.dtype)
-    put_kv.wait()
-    put_out.wait()
+    vout_v[0] = final[0:draft, :].astype(vout_v.dtype)
+    put_vout = put(vout_v, verify_out)
+    for copy in (put_kv, put_vkv, put_out, put_vout):
+        copy.wait()
+
+
+def write_out(*refs):
+    count = len(refs) // 2
+    sems = refs[-1]
+    copies = [
+        pltpu.make_async_copy(refs[k], refs[count + k], sems.at[k]) for k in range(count)
+    ]
+    for copy in copies:
+        copy.start()
+    for copy in copies:
+        copy.wait()
 
 
 def on_device(
@@ -316,11 +342,9 @@
     page = page_pool.shape[1:]
     table, high = rope_tables(pages * page[0] + draft)
     bf16, f32 = jnp.bfloat16, jnp.float32
-    smem = pl.BlockSpec(memory_space=pltpu.SMEM)
-    vmem = pl.BlockSpec(memory_space=pltpu.VMEM)
-    hbm = pl.BlockSpec(memory_space=pl.ANY)
-    fetched = 14 + heads
-    return pl.pallas_call(
+    hbm = pl.BlockSpec(memory_space=pltpu.HBM)
+    moved = 21 + heads
+    results = pl.pallas_call(
         functools.partial(kernel, n),
         out_shape=(
             jax.ShapeDtypeStruct((1, draft, half), bf16),
@@ -328,9 +352,15 @@
             jax.ShapeDtypeStruct((1, draft, 2 * HEAD), bf16),
             jax.ShapeDtypeStruct((rows, 2 * HEAD), bf16),
         ),
-        in_specs=[smem] * 5 + [vmem] + [hbm] * 10,
-        out_specs=(vmem, hbm, vmem, hbm),
+        in_specs=[hbm] * 16,
+        out_specs=(hbm,) * 4,
         scratch_shapes=[
+            pltpu.SMEM(outbound.shape, jnp.int32),
+            pltpu.SMEM(page_table.shape, jnp.int32),
+            pltpu.SMEM((1, 1), jnp.int32),
+            pltpu.SMEM(prompt_len.shape, jnp.int32),
+            pltpu.SMEM((1, 1), jnp.int32),
+            pltpu.VMEM(verify_x.shape, bf16),
             pltpu.VMEM((rows, width), bf16),
             pltpu.VMEM((PAD, width), f32),
             pltpu.VMEM((1, width), f32),
@@ -360,14 +390,16 @@
             pltpu.VMEM((2, PAD, half), f32),
             pltpu.VMEM((2, PAD, half), f32),
             pltpu.VMEM((rows, half), bf16),
-            pltpu.SemaphoreType.DMA((fetched,)),
+            pltpu.VMEM((1, draft, half), bf16),
+            pltpu.VMEM((1, draft, 2 * HEAD), bf16),
+            pltpu.SemaphoreType.DMA((moved,)),
             pltpu.SemaphoreType.DMA((n,)),
             pltpu.SemaphoreType.DMA((n,)),
             pltpu.SemaphoreType.DMA((3,)),
             pltpu.SemaphoreType.DMA((3,)),
         ],
         compiler_params=pltpu.CompilerParams(
-            collective_id=0, has_side_effects=True, vmem_limit_bytes=48 * 1024 * 1024
+            collective_id=0, has_side_effects=True, vmem_limit_bytes=VMEM_LIMIT
         ),
         cost_estimate=pl.CostEstimate(
             flops=2 * all_rows * width * (2 * columns + 2 * HEAD),
@@ -375,10 +407,18 @@
             transcendentals=heads * rows * rows,
         ),
     )(
-        outbound, page_table, cache_len, prompt_len, accepted,
+        outbound, page_table, cache_len[None], prompt_len, accepted[None],
         verify_x, prefill_x, attn_gain.reshape(1, -1), w_query, w_keyval, qk_gain, w_out,
         post_gain.reshape(1, -1), page_pool, jnp.asarray(table), jnp.asarray(high),
     )
+    return pl.pallas_call(
+        write_out,
+        out_shape=tuple(jax.ShapeDtypeStruct(r.shape, r.dtype) for r in results),
+        in_specs=[pl.BlockSpec(memory_space=pl.ANY)] * 4,
+        out_specs=(hbm,) * 4,
+        scratch_shapes=[pltpu.SemaphoreType.DMA((4,))],
+        compiler_params=pltpu.CompilerParams(vmem_limit_bytes=VMEM_LIMIT),
+    )(*results)
 
 
 def solution(mesh):

time: 36.7 us -> 49 us (1.34)
  Pallas kernels: 21 us -> 46.9 us
  local copies, waits for them, and re-layouts: 13.2 us -> 0 us
    pallas_call x0 -> x1, Pallas kernels: none -> 25.7 us  [on_device(): pl.pallas_call(write_out, out_shape=tuple((jax.ShapeDtypeStruct(r.shape,...]
    unnamed x28 -> x0, local copies, waits for them, and re-layouts: 13.2 us -> none
where the time goes in v2:
time: 49 us; the launch traced here: 48.8 us
  Pallas kernels  46.9 us (96%)
  between operations  1.94 us (4%)
    pallas_call x1, Pallas kernels, on_device(): pl.pallas_call(write_out, out_shape=tuple((jax.ShapeDtypeStruct(r.shape,...  25.7 us
    pallas_call x1, Pallas kernels, on_device(): pl.pallas_call(functools.partial(kernel, n), out_shape=(jax.ShapeDtypeStr...  21.2 us

profile of v2, /device:TPU:0, one launch (start us, length us, event | category | flops | bytes accessed | tf_op | source)
XLA Modules:
  0.0 48.8 jit_solution(14853155215325493215)
XLA Ops:
  1.9 21.2 %shard_map.183 = (bf16[1,5,1024]{2,1,0:T(8,128)(2,1)}, bf16[256,1024]{1,0:T(8,128)(2,1)}, bf16[1,5,512]{2,1,0:T(8,128)(2,1)}, bf16[256,512]{1,0:T(8,128)(2,1)}) custom-call(s32[1,16]{1,0:T(1,128)} %outbound_h.1, s32[1,64]{1,0:T(1,128)} %page_table_h.1, s32[1,1]{1,0:T(1,128)} %bitcast.4.cache_len_h, s32[1,4]{1,0:T(1,128)} %prompt_len_h.1, ...), custom_call_target="tpu_custom_call" | custom-call | flops 2852126720 | bytes 16777216 | tf_op jit(solution)/shard_map/pallas_call | solution.py:347
  23.1 25.7 %shard_map.184 = (bf16[1,5,1024]{2,1,0:T(8,128)(2,1)}, bf16[256,1024]{1,0:T(8,128)(2,1)}, bf16[1,5,512]{2,1,0:T(8,128)(2,1)}, bf16[256,512]{1,0:T(8,128)(2,1)}) custom-call(bf16[1,5,1024]{2,1,0:T(8,128)(2,1)} %get-tuple-element.8.refs_0_, bf16[256,1024]{1,0:T(8,128)(2,1)} %get-tuple-element.9.refs_1_, bf16[1,5,512]{2,1,0:T(8,128)(2,1)} %get-tuple-element.10.refs_2_, ...), custom_call_target="tpu_custom_call" | custom-call | tf_op jit(solution)/shard_map/pallas_call | solution.py:414

commit v3 on v2

--- a/solution.py
+++ b/solution.py
@@ -88,11 +88,10 @@
         return copy
 
     put = fetch
+    got_again = fetch(attn_gain, again_v)
+    got_verify = fetch(verify_h, verify_x)
+    got_x = fetch(prefill_x, x_v)
     got_outbound = fetch(outbound_h, outbound)
-    got_pool = fetch(page_pool, pool_v)
-    got_verify = fetch(verify_h, verify_x)
-    got_again = fetch(attn_gain, again_v)
-    got_x = fetch(prefill_x, x_v)
     got_small = [
         fetch(prompt_len_h, prompt_len),
         fetch(cache_len_h, cache_len),
@@ -100,6 +99,7 @@
         fetch(page_table_h, page_table),
     ]
     got_w = [fetch(w_keyval.at[:, pl.ds(i * HEAD, HEAD)], wp_v.at[i]) for i in range(2)]
+    got_pool = fetch(page_pool, pool_v)
     got_table = fetch(table, table_v)
     got_high = fetch(high, high_v)
     got_qkgain = fetch(qk_gain, qkgain_v)
@@ -112,39 +112,11 @@
     ]
     got_pgain = fetch(post_gain, pgain_v)
 
-    arrived[me] = jnp.zeros(arrived.shape[1:], arrived.dtype)
-    got_outbound.wait()
-    got_pool.wait()
-
-    def pack(d, carry):
-        page = outbound[0, d]
-        body = pool_v[jnp.clip(page, 0, pool_pages - 1)]
-        leaving[d] = lax.select(page >= 0, body, jnp.zeros_like(body))
-        return carry
-
-    lax.fori_loop(0, n, pack, 0)
-
     vx_v[...] = jnp.zeros_like(vx_v)
     got_verify.wait()
     got_again.wait()
     vx_v[0:draft, :] = verify_x[0].astype(jnp.float32)
     normed[rows:, :] = (rms(vx_v[...]) * again_v[...]).astype(jnp.bfloat16)
-
-    pl.semaphore_wait(barrier, n)
-
-    def send(step, carry):
-        d = lax.rem(me + step, n)
-        pltpu.make_async_remote_copy(
-            src_ref=leaving.at[d],
-            dst_ref=arrived.at[me],
-            send_sem=page_send.at[d],
-            recv_sem=page_recv.at[me],
-            device_id=(d, side),
-            device_id_type=MESH,
-        ).start()
-        return carry
-
-    lax.fori_loop(1, n, send, 0)
 
     got_x.wait()
     block = 32
@@ -212,10 +184,48 @@
     vkv_v[0] = vkv[0:draft, :]
     put_vkv = put(vkv_v, verify_kv)
 
-    for i in range(heads):
-        got_w[2 + i].wait()
+    arrived[me] = jnp.zeros(arrived.shape[1:], arrived.dtype)
+    got_outbound.wait()
+    got_pool.wait()
+
+    def pack(d, carry):
+        page = outbound[0, d]
+        body = pool_v[jnp.clip(page, 0, pool_pages - 1)]
+        leaving[d] = lax.select(page >= 0, body, jnp.zeros_like(body))
+        return carry
+
+    lax.fori_loop(0, n, pack, 0)
+
+    for copy in got_w[2:]:
+        copy.wait()
+
+    def project(i):
         query = rope(rms(dot(normed[...], wp_v[2 + i])) * qkgain_v[0:1, :])
         qv_v[i * PAD:(i + 1) * PAD, :] = query[rows:, :]
+        return query
+
+    ahead = project(0)
+
+    pl.semaphore_wait(barrier, n)
+
+    def send(step, carry):
+        d = lax.rem(me + step, n)
+        pltpu.make_async_remote_copy(
+            src_ref=leaving.at[d],
+            dst_ref=arrived.at[me],
+            send_sem=page_send.at[d],
+            recv_sem=page_recv.at[me],
+            device_id=(d, side),
+            device_id_type=MESH,
+        ).start()
+        return carry
+
+    lax.fori_loop(1, n, send, 0)
+
+    for i in range(heads):
+        query = ahead
+        if i + 1 < heads:
+            ahead = project(i + 1)
         scores = dot_t(query[:rows, :], kv_v[:rows, :HEAD]) + bias[...]
         weights = jnp.exp(scores - jnp.max(scores, axis=-1, keepdims=True))
         share = 1.0 / jnp.sum(weights, axis=-1, keepdims=True)
@@ -315,15 +325,17 @@
         copy.wait()
 
 
-def write_out(*refs):
-    count = len(refs) // 2
-    sems = refs[-1]
-    copies = [
-        pltpu.make_async_copy(refs[k], refs[count + k], sems.at[k]) for k in range(count)
-    ]
-    for copy in copies:
+def write_out(count, *refs):
+    sources, results, held = refs[:count], refs[count:2 * count], refs[2 * count:3 * count]
+    in_sem, out_sem = refs[3 * count:]
+    ins = [pltpu.make_async_copy(sources[k], held[k], in_sem.at[k]) for k in range(count)]
+    outs = [pltpu.make_async_copy(held[k], results[k], out_sem.at[k]) for k in range(count)]
+    for copy in ins:
         copy.start()
-    for copy in copies:
+    for k in range(count):
+        ins[k].wait()
+        outs[k].start()
+    for copy in outs:
         copy.wait()
 
 
@@ -412,11 +424,12 @@
         post_gain.reshape(1, -1), page_pool, jnp.asarray(table), jnp.asarray(high),
     )
     return pl.pallas_call(
-        write_out,
+        functools.partial(write_out, len(results)),
         out_shape=tuple(jax.ShapeDtypeStruct(r.shape, r.dtype) for r in results),
         in_specs=[pl.BlockSpec(memory_space=pl.ANY)] * 4,
         out_specs=(hbm,) * 4,
-        scratch_shapes=[pltpu.SemaphoreType.DMA((4,))],
+        scratch_shapes=[pltpu.VMEM(r.shape, r.dtype) for r in results]
+        + [pltpu.SemaphoreType.DMA((len(results),))] * 2,
         compiler_params=pltpu.CompilerParams(vmem_limit_bytes=VMEM_LIMIT),
     )(*results)
 

time: 49 us -> 24.3 us (0.50)
  Pallas kernels: 46.9 us -> 22.1 us
    pallas_call x1, Pallas kernels: 25.7 us -> 2.01 us  [on_device(): pl.pallas_call(functools.partial(write_out, len(results)), out_shape=tupl...]
    pallas_call x1, Pallas kernels: 21.2 us -> 20.1 us  [on_device(): pl.pallas_call(functools.partial(kernel, n), out_shape=(jax.ShapeDtypeStr...]
where the time goes in v3:
time: 24.3 us; the launch traced here: 24 us
  Pallas kernels  22.1 us (91%)
  between operations  1.94 us (8%)
    pallas_call x1, Pallas kernels, on_device(): pl.pallas_call(functools.partial(kernel, n), out_shape=(jax.ShapeDtypeStr...  20.1 us
    pallas_call x1, Pallas kernels, on_device(): pl.pallas_call(functools.partial(write_out, len(results)), out_shape=tupl...  2.01 us

profile of v3, /device:TPU:0, one launch (start us, length us, event | category | flops | bytes accessed | tf_op | source)
XLA Modules:
  0.0 24.0 jit_solution(1454043118755783444)
XLA Ops:
  1.9 20.1 %shard_map.183 = (bf16[1,5,1024]{2,1,0:T(8,128)(2,1)}, bf16[256,1024]{1,0:T(8,128)(2,1)}, bf16[1,5,512]{2,1,0:T(8,128)(2,1)}, bf16[256,512]{1,0:T(8,128)(2,1)}) custom-call(s32[1,16]{1,0:T(1,128)} %outbound_h.1, s32[1,64]{1,0:T(1,128)} %page_table_h.1, s32[1,1]{1,0:T(1,128)} %bitcast.4.cache_len_h, s32[1,4]{1,0:T(1,128)} %prompt_len_h.1, ...), custom_call_target="tpu_custom_call" | custom-call | flops 2852126720 | bytes 16777216 | tf_op jit(solution)/shard_map/pallas_call | solution.py:359
  22.0 2.0 %shard_map.184 = (bf16[1,5,1024]{2,1,0:T(8,128)(2,1)}, bf16[256,1024]{1,0:T(8,128)(2,1)}, bf16[1,5,512]{2,1,0:T(8,128)(2,1)}, bf16[256,512]{1,0:T(8,128)(2,1)}) custom-call(bf16[1,5,1024]{2,1,0:T(8,128)(2,1)} %get-tuple-element.8.refs_0_, bf16[256,1024]{1,0:T(8,128)(2,1)} %get-tuple-element.9.refs_1_, bf16[1,5,512]{2,1,0:T(8,128)(2,1)} %get-tuple-element.10.refs_2_, ...), custom_call_target="tpu_custom_call" | custom-call | tf_op jit(solution)/shard_map/pallas_call | solution.py:426

commit v4 on v3

--- a/solution.py
+++ b/solution.py
@@ -49,7 +49,7 @@
     verify_h, prefill_x, attn_gain, w_query, w_keyval, qk_gain, w_out, post_gain,
     page_pool, table, high,
     verify_out, prefill_out, verify_kv, prefill_kv,
-    outbound, page_table, cache_len, prompt_len, accepted, verify_x,
+    outbound, page_table, cache_len, prompt_len, accepted, verify_x, table_row,
     x_v, vx_v, again_v, pgain_v, qkgain_v, table_v, high_v,
     wp_v, wo_v, pool_v, leaving, arrived, cached,
     normed, cos_v, sin_v, bias, kv_v, qv_v, attn_v, vattn_v,
@@ -97,6 +97,7 @@
         fetch(cache_len_h, cache_len),
         fetch(accepted_h, accepted),
         fetch(page_table_h, page_table),
+        fetch(page_table_h, table_row),
     ]
     got_w = [fetch(w_keyval.at[:, pl.ds(i * HEAD, HEAD)], wp_v.at[i]) for i in range(2)]
     got_pool = fetch(page_pool, pool_v)
@@ -119,14 +120,17 @@
     normed[rows:, :] = (rms(vx_v[...]) * again_v[...]).astype(jnp.bfloat16)
 
     got_x.wait()
-    block = 32
+    block = 16
 
     def norm_rows(i, carry):
-        at = pl.ds(pl.multiple_of(i * block, block), block)
-        normed[at, :] = (rms(x_v[at, :].astype(jnp.float32)) * again_v[...]).astype(jnp.bfloat16)
-        return carry
-
-    lax.fori_loop(0, rows // block, norm_rows, 0)
+        for u in range(4):
+            at = pl.ds(pl.multiple_of(i * 4 * block, block) + u * block, block)
+            normed[at, :] = (
+                rms(x_v[at, :].astype(jnp.float32)) * again_v[...]
+            ).astype(jnp.bfloat16)
+        return carry
+
+    lax.fori_loop(0, rows // (4 * block), norm_rows, 0)
 
     for copy in got_small:
         copy.wait()
@@ -188,23 +192,14 @@
     got_outbound.wait()
     got_pool.wait()
 
-    def pack(d, carry):
-        page = outbound[0, d]
-        body = pool_v[jnp.clip(page, 0, pool_pages - 1)]
-        leaving[d] = lax.select(page >= 0, body, jnp.zeros_like(body))
-        return carry
-
-    lax.fori_loop(0, n, pack, 0)
-
-    for copy in got_w[2:]:
-        copy.wait()
-
-    def project(i):
-        query = rope(rms(dot(normed[...], wp_v[2 + i])) * qkgain_v[0:1, :])
-        qv_v[i * PAD:(i + 1) * PAD, :] = query[rows:, :]
-        return query
-
-    ahead = project(0)
+    def pack(i, carry):
+        for u in range(4):
+            page = outbound[0, i * 4 + u]
+            body = pool_v[jnp.clip(page, 0, pool_pages - 1)]
+            leaving[i * 4 + u] = lax.select(page >= 0, body, jnp.zeros_like(body))
+        return carry
+
+    lax.fori_loop(0, n // 4, pack, 0)
 
     pl.semaphore_wait(barrier, n)
 
@@ -221,6 +216,16 @@
         return carry
 
     lax.fori_loop(1, n, send, 0)
+
+    for copy in got_w[2:]:
+        copy.wait()
+
+    def project(i):
+        query = rope(rms(dot(normed[...], wp_v[2 + i])) * qkgain_v[0:1, :])
+        qv_v[i * PAD:(i + 1) * PAD, :] = query[rows:, :]
+        return query
+
+    ahead = project(0)
 
     for i in range(heads):
         query = ahead
@@ -250,6 +255,66 @@
     got_wo[1].wait()
     own_v[...] = dot(attn_v[...], wo_v[1])
 
+    group = 8
+
+    def gather(i, carry):
+        for u in range(group):
+            page = page_table[0, i * group + u]
+            at = pl.ds(pl.multiple_of(i * group * page_rows, page_rows) + u * page_rows, page_rows)
+            cached[at, :] = pool_v[jnp.clip(page, 0, pool_pages - 1)]
+        return carry
+
+    lax.fori_loop(0, pages // group, gather, 0)
+    square_row = lax.broadcasted_iota(jnp.int32, (pages, pages), 0)
+    square_col = lax.broadcasted_iota(jnp.int32, (pages, pages), 1)
+    spread = jnp.broadcast_to(table_row[...], (pages, pages))
+    page_col = jnp.sum(
+        jnp.where(square_row == square_col, spread, 0), axis=1, keepdims=True
+    )
+    slots = pages * page_rows
+    slot_page = lax.broadcasted_iota(jnp.int32, (pages, slots), 0) * page_rows
+    slot = lax.broadcasted_iota(jnp.int32, (pages, slots), 1)
+    here = (slot >= slot_page) & (slot < slot_page + page_rows)
+    here = here & (page_col < pool_pages) & (slot < length)
+    here = jnp.sum(jnp.where(here, 1.0, 0.0), axis=0, keepdims=True)
+    came = n * page_rows
+    came_row = lax.broadcasted_iota(jnp.int32, (pages, came), 1)
+    came_page = lax.shift_right_logical(came_row, page_rows.bit_length() - 1)
+    came_slot = lax.broadcasted_iota(jnp.int32, (pages, came), 0) * page_rows
+    came_slot = came_slot + came_row - came_page * page_rows
+    uses = (page_col == came_page + pool_pages) & (came_slot < length)
+    uses = jnp.sum(jnp.where(uses, 1.0, 0.0), axis=0, keepdims=True)
+
+    swap_rows.wait()
+    summed = own_v[...] + got_v[...].astype(jnp.float32)
+    own_v[...] = summed
+    stat_v[...] = jnp.broadcast_to(jnp.sum(summed * summed, axis=-1, keepdims=True), stat_v.shape)
+    swap_stat = swap(stat_v, gstat_v, 1)
+
+    queries = qv_v[...]
+    old = jnp.where(here > 0.0, dot_t(queries, cached[:, :HEAD]), neg_large)
+    new = dot_t(queries, kv_v[rows:, :HEAD])
+    step = jnp.bitwise_and(lax.broadcasted_iota(jnp.int32, new.shape, 0), PAD - 1)
+    new = jnp.where(lax.broadcasted_iota(jnp.int32, new.shape, 1) <= step, new, neg_large)
+    peak = jnp.maximum(
+        jnp.max(old, axis=-1, keepdims=True), jnp.max(new, axis=-1, keepdims=True)
+    )
+    old = jnp.exp(old - peak)
+    new = jnp.exp(new - peak)
+    total = jnp.sum(old, axis=-1, keepdims=True) + jnp.sum(new, axis=-1, keepdims=True)
+    mixed = dot(old.astype(jnp.bfloat16), cached[:, HEAD:])
+    mixed = mixed + dot(new.astype(jnp.bfloat16), kv_v[rows:, HEAD:])
+
+    got_pgain.wait()
+    gain = pgain_v[:, pl.ds(mine, half)]
+    swap_stat.wait()
+    square = stat_v[:, 0:1] + gstat_v[:, 0:1]
+    scale = lax.rsqrt(square / width + eps_norm)
+    out_v[...] = (
+        x_v[:, pl.ds(mine, half)].astype(jnp.float32) + own_v[...] * scale * gain
+    ).astype(out_v.dtype)
+    put_out = put(out_v, prefill_out)
+
     def arrive(step, carry):
         s = lax.rem(me + n - step, n)
         pltpu.make_async_remote_copy(
@@ -264,54 +329,21 @@
 
     lax.fori_loop(1, n, arrive, 0)
 
-    def gather(i, carry):
-        page = page_table[0, i]
-        local = pool_v[jnp.minimum(page, pool_pages - 1)]
-        moved = arrived[jnp.clip(page - pool_pages, 0, n - 1)]
-        at = pl.ds(pl.multiple_of(i * page_rows, page_rows), page_rows)
-        cached[at, :] = lax.select(page < pool_pages, local, moved)
-        return carry
-
-    lax.fori_loop(0, pages, gather, 0)
-
-    queries = qv_v[...]
-    old = dot_t(queries, cached[:, :HEAD])
-    slot = lax.broadcasted_iota(jnp.int32, old.shape, 1)
-    old = jnp.where(slot < length, old, neg_large)
-    new = dot_t(queries, kv_v[rows:, :HEAD])
-    step = jnp.bitwise_and(lax.broadcasted_iota(jnp.int32, new.shape, 0), PAD - 1)
-    new = jnp.where(lax.broadcasted_iota(jnp.int32, new.shape, 1) <= step, new, neg_large)
-    peak = jnp.maximum(
-        jnp.max(old, axis=-1, keepdims=True), jnp.max(new, axis=-1, keepdims=True)
-    )
-    old = jnp.exp(old - peak)
-    new = jnp.exp(new - peak)
-    share = 1.0 / (jnp.sum(old, axis=-1, keepdims=True) + jnp.sum(new, axis=-1, keepdims=True))
-    mixed = dot((old * share).astype(jnp.bfloat16), cached[:, HEAD:])
-    mixed = mixed + dot((new * share).astype(jnp.bfloat16), kv_v[rows:, HEAD:])
-    mixed = mixed.astype(jnp.bfloat16)
+
+    moved = arrived[...].reshape(came, 2 * HEAD)
+    scores = jnp.where(uses > 0.0, dot_t(queries, moved[:, :HEAD]), neg_large)
+    top = jnp.maximum(peak, jnp.max(scores, axis=-1, keepdims=True))
+    weights = uses * jnp.exp(scores - top)
+    keep = jnp.exp(peak - top)
+    total = total * keep + jnp.sum(weights, axis=-1, keepdims=True)
+    mixed = mixed * keep + dot(weights.astype(jnp.bfloat16), moved[:, HEAD:])
+    mixed = (mixed * (1.0 / total)).astype(jnp.bfloat16)
     for i in range(heads):
         vattn_v[:, i * HEAD:(i + 1) * HEAD] = mixed[i * PAD:(i + 1) * PAD, :]
-
-    swap_rows.wait()
-    summed = own_v[...] + got_v[...].astype(jnp.float32)
-    own_v[...] = summed
-    stat_v[...] = jnp.broadcast_to(jnp.sum(summed * summed, axis=-1, keepdims=True), stat_v.shape)
-    swap_stat = swap(stat_v, gstat_v, 1)
 
     vsend_v[0] = dot(vattn_v[...], wo_v[0])
     vsend_v[1] = dot(vattn_v[...], wo_v[1])
     swap_verify = swap(vsend_v, vgot_v, 2)
-
-    got_pgain.wait()
-    gain = pgain_v[:, pl.ds(mine, half)]
-    swap_stat.wait()
-    square = stat_v[:, 0:1] + gstat_v[:, 0:1]
-    scale = lax.rsqrt(square / width + eps_norm)
-    out_v[...] = (
-        x_v[:, pl.ds(mine, half)].astype(jnp.float32) + own_v[...] * scale * gain
-    ).astype(out_v.dtype)
-    put_out = put(out_v, prefill_out)
 
     swap_verify.wait()
     ours = vsend_v[1] + vgot_v[0]
@@ -355,7 +387,7 @@
     table, high = rope_tables(pages * page[0] + draft)
     bf16, f32 = jnp.bfloat16, jnp.float32
     hbm = pl.BlockSpec(memory_space=pltpu.HBM)
-    moved = 21 + heads
+    moved = 22 + heads
     results = pl.pallas_call(
         functools.partial(kernel, n),
         out_shape=(
@@ -373,6 +405,7 @@
             pltpu.SMEM(prompt_len.shape, jnp.int32),
             pltpu.SMEM((1, 1), jnp.int32),
             pltpu.VMEM(verify_x.shape, bf16),
+            pltpu.VMEM(page_table.shape, jnp.int32),
             pltpu.VMEM((rows, width), bf16),
             pltpu.VMEM((PAD, width), f32),
             pltpu.VMEM((1, width), f32),

time: 24.3 us -> 22 us (0.905)
  Pallas kernels: 22.1 us -> 19.8 us
    pallas_call x1, Pallas kernels: 20.1 us -> 17.8 us  [on_device(): pl.pallas_call(functools.partial(kernel, n), out_shape=(jax.ShapeDtypeStr...]
where the time goes in v4:
time: 22 us; the launch traced here: 21.7 us
  Pallas kernels  19.8 us (90%)
  between operations  1.94 us (9%)
    pallas_call x1, Pallas kernels, on_device(): pl.pallas_call(functools.partial(kernel, n), out_shape=(jax.ShapeDtypeStr...  17.8 us
    pallas_call x1, Pallas kernels, on_device(): pl.pallas_call(functools.partial(write_out, len(results)), out_shape=tupl...  2.01 us

profile of v4, /device:TPU:0, one launch (start us, length us, event | category | flops | bytes accessed | tf_op | source)
XLA Modules:
  0.0 21.7 jit_solution(4889121590320317641)
XLA Ops:
  1.9 17.8 %shard_map.183 = (bf16[1,5,1024]{2,1,0:T(8,128)(2,1)}, bf16[256,1024]{1,0:T(8,128)(2,1)}, bf16[1,5,512]{2,1,0:T(8,128)(2,1)}, bf16[256,512]{1,0:T(8,128)(2,1)}) custom-call(s32[1,16]{1,0:T(1,128)} %outbound_h.1, s32[1,64]{1,0:T(1,128)} %page_table_h.1, s32[1,1]{1,0:T(1,128)} %bitcast.4.cache_len_h, s32[1,4]{1,0:T(1,128)} %prompt_len_h.1, ...), custom_call_target="tpu_custom_call" | custom-call | flops 2852126720 | bytes 16777216 | tf_op jit(solution)/shard_map/pallas_call | solution.py:391
  19.7 2.0 %shard_map.184 = (bf16[1,5,1024]{2,1,0:T(8,128)(2,1)}, bf16[256,1024]{1,0:T(8,128)(2,1)}, bf16[1,5,512]{2,1,0:T(8,128)(2,1)}, bf16[256,512]{1,0:T(8,128)(2,1)}) custom-call(bf16[1,5,1024]{2,1,0:T(8,128)(2,1)} %get-tuple-element.8.refs_0_, bf16[256,1024]{1,0:T(8,128)(2,1)} %get-tuple-element.9.refs_1_, bf16[1,5,512]{2,1,0:T(8,128)(2,1)} %get-tuple-element.10.refs_2_, ...), custom_call_target="tpu_custom_call" | custom-call | tf_op jit(solution)/shard_map/pallas_call | solution.py:459

commit v5 on v4

--- a/solution.py
+++ b/solution.py
@@ -68,17 +68,6 @@
     mine = pl.multiple_of(side * half, half)
     theirs = pl.multiple_of((1 - side) * half, half)
 
-    barrier = pltpu.get_barrier_semaphore()
-    pl.semaphore_signal(barrier, inc=1, device_id=(me, 1 - side), device_id_type=MESH)
-
-    def greet(step, carry):
-        pl.semaphore_signal(
-            barrier, inc=1, device_id=(lax.rem(me + step, n), side), device_id_type=MESH
-        )
-        return carry
-
-    lax.fori_loop(1, n, greet, 0)
-
     copies = []
 
     def fetch(src, dst):
@@ -92,6 +81,19 @@
     got_verify = fetch(verify_h, verify_x)
     got_x = fetch(prefill_x, x_v)
     got_outbound = fetch(outbound_h, outbound)
+    got_pool = fetch(page_pool, pool_v)
+
+    barrier = pltpu.get_barrier_semaphore()
+    pl.semaphore_signal(barrier, inc=1, device_id=(me, 1 - side), device_id_type=MESH)
+
+    def greet(step, carry):
+        pl.semaphore_signal(
+            barrier, inc=1, device_id=(lax.rem(me + step, n), side), device_id_type=MESH
+        )
+        return carry
+
+    lax.fori_loop(1, n, greet, 0)
+
     got_small = [
         fetch(prompt_len_h, prompt_len),
         fetch(cache_len_h, cache_len),
@@ -100,7 +102,6 @@
         fetch(page_table_h, table_row),
     ]
     got_w = [fetch(w_keyval.at[:, pl.ds(i * HEAD, HEAD)], wp_v.at[i]) for i in range(2)]
-    got_pool = fetch(page_pool, pool_v)
     got_table = fetch(table, table_v)
     got_high = fetch(high, high_v)
     got_qkgain = fetch(qk_gain, qkgain_v)
@@ -131,6 +132,35 @@
         return carry
 
     lax.fori_loop(0, rows // (4 * block), norm_rows, 0)
+
+    arrived[me] = jnp.zeros(arrived.shape[1:], arrived.dtype)
+    got_outbound.wait()
+    got_pool.wait()
+
+    def pack(i, carry):
+        for u in range(4):
+            page = outbound[0, i * 4 + u]
+            body = pool_v[jnp.clip(page, 0, pool_pages - 1)]
+            leaving[i * 4 + u] = lax.select(page >= 0, body, jnp.zeros_like(body))
+        return carry
+
+    lax.fori_loop(0, n // 4, pack, 0)
+
+    pl.semaphore_wait(barrier, n)
+
+    def send(step, carry):
+        d = lax.rem(me + step, n)
+        pltpu.make_async_remote_copy(
+            src_ref=leaving.at[d],
+            dst_ref=arrived.at[me],
+            send_sem=page_send.at[d],
+            recv_sem=page_recv.at[me],
+            device_id=(d, side),
+            device_id_type=MESH,
+        ).start()
+        return carry
+
+    lax.fori_loop(1, n, send, 0)
 
     for copy in got_small:
         copy.wait()
@@ -187,35 +217,6 @@
     vkv = jnp.where(vrow < accepted[0, 0], vkv, 0.0).astype(jnp.bfloat16)
     vkv_v[0] = vkv[0:draft, :]
     put_vkv = put(vkv_v, verify_kv)
-
-    arrived[me] = jnp.zeros(arrived.shape[1:], arrived.dtype)
-    got_outbound.wait()
-    got_pool.wait()
-
-    def pack(i, carry):
-        for u in range(4):
-            page = outbound[0, i * 4 + u]
-            body = pool_v[jnp.clip(page, 0, pool_pages - 1)]
-            leaving[i * 4 + u] = lax.select(page >= 0, body, jnp.zeros_like(body))
-        return carry
-
-    lax.fori_loop(0, n // 4, pack, 0)
-
-    pl.semaphore_wait(barrier, n)
-
-    def send(step, carry):
-        d = lax.rem(me + step, n)
-        pltpu.make_async_remote_copy(
-            src_ref=leaving.at[d],
-            dst_ref=arrived.at[me],
-            send_sem=page_send.at[d],
-            recv_sem=page_recv.at[me],
-            device_id=(d, side),
-            device_id_type=MESH,
-        ).start()
-        return carry
-
-    lax.fori_loop(1, n, send, 0)
 
     for copy in got_w[2:]:
         copy.wait()

time: 22 us -> 23.4 us (1.064)
  Pallas kernels: 19.8 us -> 21.2 us
    pallas_call x1, Pallas kernels: 17.8 us -> 19.2 us  [on_device(): pl.pallas_call(functools.partial(kernel, n), out_shape=(jax.ShapeDtypeStr...]
where the time goes in v5:
time: 23.4 us; the launch traced here: 23.1 us
  Pallas kernels  21.2 us (91%)
  between operations  1.94 us (8%)
    pallas_call x1, Pallas kernels, on_device(): pl.pallas_call(functools.partial(kernel, n), out_shape=(jax.ShapeDtypeStr...  19.2 us
    pallas_call x1, Pallas kernels, on_device(): pl.pallas_call(functools.partial(write_out, len(results)), out_shape=tupl...  2.01 us

profile of v5, /device:TPU:0, one launch (start us, length us, event | category | flops | bytes accessed | tf_op | source)
XLA Modules:
  0.0 23.1 jit_solution(2155936482210164115)
XLA Ops:
  1.9 19.2 %shard_map.183 = (bf16[1,5,1024]{2,1,0:T(8,128)(2,1)}, bf16[256,1024]{1,0:T(8,128)(2,1)}, bf16[1,5,512]{2,1,0:T(8,128)(2,1)}, bf16[256,512]{1,0:T(8,128)(2,1)}) custom-call(s32[1,16]{1,0:T(1,128)} %outbound_h.1, s32[1,64]{1,0:T(1,128)} %page_table_h.1, s32[1,1]{1,0:T(1,128)} %bitcast.4.cache_len_h, s32[1,4]{1,0:T(1,128)} %prompt_len_h.1, ...), custom_call_target="tpu_custom_call" | custom-call | flops 2852126720 | bytes 16777216 | tf_op jit(solution)/shard_map/pallas_call | solution.py:392
  21.1 2.0 %shard_map.184 = (bf16[1,5,1024]{2,1,0:T(8,128)(2,1)}, bf16[256,1024]{1,0:T(8,128)(2,1)}, bf16[1,5,512]{2,1,0:T(8,128)(2,1)}, bf16[256,512]{1,0:T(8,128)(2,1)}) custom-call(bf16[1,5,1024]{2,1,0:T(8,128)(2,1)} %get-tuple-element.8.refs_0_, bf16[256,1024]{1,0:T(8,128)(2,1)} %get-tuple-element.9.refs_1_, bf16[1,5,512]{2,1,0:T(8,128)(2,1)} %get-tuple-element.10.refs_2_, ...), custom_call_target="tpu_custom_call" | custom-call | tf_op jit(solution)/shard_map/pallas_call | solution.py:460

commit v6 on v4

--- a/solution.py
+++ b/solution.py
@@ -180,14 +180,6 @@
 
     got_w[0].wait()
     kv_v[:, :HEAD] = rope(rms(dot(normed[...], wp_v[0])) * qkgain_v[1:2, :])
-    got_w[1].wait()
-    kv_v[:, HEAD:] = rms(dot(normed[...], wp_v[1])).astype(jnp.bfloat16)
-    put_kv = put(kv_v.at[pl.ds(0, rows)], prefill_kv)
-    vkv = kv_v[rows:, :].astype(jnp.float32)
-    vkv = jnp.where(vrow < accepted[0, 0], vkv, 0.0).astype(jnp.bfloat16)
-    vkv_v[0] = vkv[0:draft, :]
-    put_vkv = put(vkv_v, verify_kv)
-
     arrived[me] = jnp.zeros(arrived.shape[1:], arrived.dtype)
     got_outbound.wait()
     got_pool.wait()
@@ -204,7 +196,8 @@
     pl.semaphore_wait(barrier, n)
 
     def send(step, carry):
-        d = lax.rem(me + step, n)
+        turn = n // 2 + (step // 2) * (1 - 2 * (step % 2))
+        d = lax.rem(me + turn, n)
         pltpu.make_async_remote_copy(
             src_ref=leaving.at[d],
             dst_ref=arrived.at[me],
@@ -216,6 +209,14 @@
         return carry
 
     lax.fori_loop(1, n, send, 0)
+
+    got_w[1].wait()
+    kv_v[:, HEAD:] = rms(dot(normed[...], wp_v[1])).astype(jnp.bfloat16)
+    put_kv = put(kv_v.at[pl.ds(0, rows)], prefill_kv)
+    vkv = kv_v[rows:, :].astype(jnp.float32)
+    vkv = jnp.where(vrow < accepted[0, 0], vkv, 0.0).astype(jnp.bfloat16)
+    vkv_v[0] = vkv[0:draft, :]
+    put_vkv = put(vkv_v, verify_kv)
 
     for copy in got_w[2:]:
         copy.wait()

time: 22 us -> 23.3 us (1.059)
  Pallas kernels: 19.8 us -> 21.1 us
    pallas_call x1, Pallas kernels: 17.8 us -> 19.1 us  [on_device(): pl.pallas_call(functools.partial(kernel, n), out_shape=(jax.ShapeDtypeStr...]
where the time goes in v6:
time: 23.3 us; the launch traced here: 23 us
  Pallas kernels  21.1 us (91%)
  between operations  1.94 us (8%)
    pallas_call x1, Pallas kernels, on_device(): pl.pallas_call(functools.partial(kernel, n), out_shape=(jax.ShapeDtypeStr...  19.1 us
    pallas_call x1, Pallas kernels, on_device(): pl.pallas_call(functools.partial(write_out, len(results)), out_shape=tupl...  2.01 us

profile of v6, /device:TPU:0, one launch (start us, length us, event | category | flops | bytes accessed | tf_op | source)
XLA Modules:
  0.0 23.0 jit_solution(13529838642679431326)
XLA Ops:
  1.9 19.1 %shard_map.183 = (bf16[1,5,1024]{2,1,0:T(8,128)(2,1)}, bf16[256,1024]{1,0:T(8,128)(2,1)}, bf16[1,5,512]{2,1,0:T(8,128)(2,1)}, bf16[256,512]{1,0:T(8,128)(2,1)}) custom-call(s32[1,16]{1,0:T(1,128)} %outbound_h.1, s32[1,64]{1,0:T(1,128)} %page_table_h.1, s32[1,1]{1,0:T(1,128)} %bitcast.4.cache_len_h, s32[1,4]{1,0:T(1,128)} %prompt_len_h.1, ...), custom_call_target="tpu_custom_call" | custom-call | flops 2852126720 | bytes 16777216 | tf_op jit(solution)/shard_map/pallas_call | solution.py:392
  21.0 2.0 %shard_map.184 = (bf16[1,5,1024]{2,1,0:T(8,128)(2,1)}, bf16[256,1024]{1,0:T(8,128)(2,1)}, bf16[1,5,512]{2,1,0:T(8,128)(2,1)}, bf16[256,512]{1,0:T(8,128)(2,1)}) custom-call(bf16[1,5,1024]{2,1,0:T(8,128)(2,1)} %get-tuple-element.8.refs_0_, bf16[256,1024]{1,0:T(8,128)(2,1)} %get-tuple-element.9.refs_1_, bf16[1,5,512]{2,1,0:T(8,128)(2,1)} %get-tuple-element.10.refs_2_, ...), custom_call_target="tpu_custom_call" | custom-call | tf_op jit(solution)/shard_map/pallas_call | solution.py:460
